TPU v7x, 256 devices: a whole 4x4x8 slice. The times are simulated.
256 devices in a mesh: ctx: 32 (over x, z), head: 8 (over y, core).
Axes of the slice: x: 4, y: 4, z: 8, core: 2. Of those that a mesh axis runs over, the one named last changes fastest.
Arguments:
- channels_in: bfloat16 [49152, 8192], P('ctx', 'head'), may hold values from -6 to 6
- state_maps: bfloat16 [49152, 2, 1024], P('ctx', None, 'head'), may hold values from -6 to 6
- gate_in: bfloat16 [49152, 8192], P('ctx', 'head'), may hold values from -6 to 6
- step_raw: float32 [49152, 128], P('ctx', 'head'), may hold values from -1.2 to 80
- convolution_channel_taps: float32 [4, 8192], P(None, 'head'), may hold values from -3 to 3
- conv_maps: float32 [4, 2, 1024], P(None, None, 'head'), may hold values from -3 to 3
- head_rates: float32 [2, 128], P(None, 'head'), may hold values from -8 to 0
- skip_gain: float32 [128], P('head'), may hold values from 0.5 to 2
- norm_gain: float32 [8192], P('head'), may hold values from 0.5 to 1.5
Outputs:
- relaid: bfloat16 [49152, 8192], P(('ctx', 'head'))
All inputs are finite; a program needn't handle non-finite values.
Results may differ from a plain program's by a relative error of at most 0.006.
Values may be sent and summed in bfloat16 or wider, within the bound.
A program may use at most 128 MiB of HBM per device.

v0:
```python
import jax
import jax.numpy as jnp
from jax import lax
from jax.sharding import PartitionSpec as P

HEAD_DIM = 64
STATE = 128
TAPS = 4
STRETCH = 256


HIGHEST_PRECISION = lax.Precision.HIGHEST
EPSILON = 1e-05


def passed_along(value, axis, by):
    peers = lax.axis_size(axis)
    pairs = [(i, i + by) for i in range(peers) if 0 <= i + by < peers]
    return lax.ppermute(value, axis, pairs)


def stretch_terms(pieces):
    values, b_maps, c_maps, step_sizes, log_rates = pieces
    length = values.shape[0]
    cumlog = jnp.cumsum(log_rates, axis=0)
    causal = jnp.arange(length)[:, None] >= jnp.arange(length)[None, :]
    log_gaps = cumlog[:, None] - cumlog[None, :]
    decays = jnp.exp(jnp.where(causal[:, :, None, None], log_gaps, -jnp.inf))
    scores = jnp.einsum("tgn,sgn->tsg", c_maps, b_maps, preferred_element_type=jnp.float32)
    weights = (scores[..., None] * decays * step_sizes[None]).astype(jnp.bfloat16)
    inside = jnp.einsum("tsgh,sghp->tghp", weights, values, preferred_element_type=jnp.float32)
    tail_weights = jnp.exp(cumlog[-1][None] - cumlog) * step_sizes
    tail = (tail_weights[..., None] * values.astype(jnp.float32)).astype(jnp.bfloat16)
    summary = jnp.einsum("sghp,sgn->ghpn", tail, b_maps, preferred_element_type=jnp.float32)
    return (inside, summary, cumlog)


def per_device(
    channels_in,
    state_maps,
    gate_in,
    step_raw,
    convolution_channel_taps,
    conv_maps,
    head_rates,
    skip_gain,
    norm_gain,
):
    count_of_rows, channel_count = channels_in.shape
    head_count = step_raw.shape[1]
    map_width = state_maps.shape[2]
    groups = map_width // STATE
    per_group = head_count // groups
    current = jnp.concatenate([channels_in, state_maps.reshape(count_of_rows, 2 * map_width)], 1)
    previous = passed_along(current[count_of_rows - (TAPS - 1) :], "ctx", 1)
    padded = jnp.concatenate([previous, current], 0).astype(jnp.float32)
    kernel = jnp.concatenate([convolution_channel_taps, conv_maps.reshape(TAPS, 2 * map_width)], 1)
    summed = jnp.zeros((count_of_rows, channel_count + 2 * map_width), jnp.float32)
    for offset in range(TAPS):
        summed = summed + kernel[offset] * padded[offset : offset + count_of_rows]
    conved = jax.nn.silu(summed).astype(jnp.bfloat16)
    stretch_count = count_of_rows // STRETCH
    values = conved[:, :channel_count].reshape(stretch_count, STRETCH, groups, per_group, HEAD_DIM)
    b_maps = conved[:, channel_count : channel_count + map_width].reshape(
        stretch_count, STRETCH, groups, STATE
    )
    c_maps = conved[:, channel_count + map_width :].reshape(stretch_count, STRETCH, groups, STATE)
    step_sizes = jax.nn.softplus(step_raw + head_rates[0][None, :])
    log_rates = -jnp.exp(head_rates[1])[None, :] * step_sizes
    step_sizes = step_sizes.reshape(stretch_count, STRETCH, groups, per_group)
    log_rates = log_rates.reshape(stretch_count, STRETCH, groups, per_group)
    inside, summary, cumlog = lax.map(
        stretch_terms, (values, b_maps, c_maps, step_sizes, log_rates)
    )
    final_logs = cumlog[:, -1]

    def advance(carried, pieces):
        final_log, summary_term = pieces
        return (jnp.exp(final_log)[..., None, None] * carried + summary_term, carried)

    initial = jnp.zeros(summary.shape[1:], jnp.float32)
    dev_state, enter_local = lax.scan(advance, initial, (final_logs, summary))
    dev_log = jnp.sum(final_logs, axis=0)
    damping = jnp.exp(dev_log)[..., None, None]

    def relay_step(stepno, carried):
        return passed_along(damping * carried + dev_state, "ctx", 1)

    incoming = lax.fori_loop(0, lax.axis_size("ctx") - 1, relay_step, jnp.zeros_like(dev_state))
    before_logs = jnp.cumsum(final_logs, axis=0) - final_logs
    entering = jnp.exp(before_logs)[..., None, None] * incoming[None] + enter_local
    c_wide = c_maps.astype(jnp.float32)
    from_state = (
        jnp.einsum("ctgn,cghpn->ctghp", c_wide, entering, precision=HIGHEST_PRECISION)
        * jnp.exp(cumlog)[..., None]
    )
    skipped = skip_gain.reshape(groups, per_group)[..., None] * values.astype(jnp.float32)
    ssm_out = (inside + from_state + skipped).reshape(count_of_rows, groups, per_group * HEAD_DIM)
    gating = jax.nn.silu(gate_in.astype(jnp.float32)).reshape(
        count_of_rows, groups, per_group * HEAD_DIM
    )
    gated_out = ssm_out * gating
    inverse_rms = lax.rsqrt(jnp.mean(gated_out * gated_out, axis=-1, keepdims=True) + EPSILON)
    normed = gated_out * inverse_rms * norm_gain.reshape(groups, per_group * HEAD_DIM)
    normed = normed.reshape(count_of_rows, channel_count).astype(jnp.bfloat16)
    return lax.all_to_all(normed, "head", split_axis=0, concat_axis=1, tiled=True)


def solution(mesh):
    return jax.shard_map(
        per_device,
        mesh=mesh,
        in_specs=(
            P("ctx", "head"),
            P("ctx", None, "head"),
            P("ctx", "head"),
            P("ctx", "head"),
            P(None, "head"),
            P(None, None, "head"),
            P(None, "head"),
            P("head"),
            P("head"),
        ),
        out_specs=P(("ctx", "head"), None),
        check_vma=False,
    )
```

profile of v0, /device:TPU:6, one launch (start us, length us, event | category | flops | bytes accessed | tf_op | source)
XLA Modules:
  0.0 659.6 jit_solution(9454736714011496196)
XLA Ops:
  42.7 44.6 %while.37 = (s32[]{:T(128)}, f32[6,256,1,16,64]{1,4,3,2,0:T(8,128)}, f32[6,1,16,64,128]{4,3,2,1,0:T(8,128)}, f32[6,256,1,16]{1,2,3,0:T(1,128)S(1)}, bf16[6,256,1...) while((s32[]{:T(128)}, ...), condition=%wide.region_3.4_spmd, body=%wide.region_0.3_spmd.sunk | while | flops 224735280 | bytes 4477953 | solution.py:72
  90.0 12.1 %while.39 = (s32[]{:T(128)}, f32[1,16,64,128]{3,2,1,0:T(8,128)S(1)}, f32[6,1,16,64,128]{4,3,2,1,0:T(8,128)}, f32[6,1,16]{2,1,0:T(1,128)S(1)}, f32[6,1,16,64,128]{4,3,2,1,0:T(8,128)}, /*index=5*/s32[]{:T(128)}, s32[]{:T(128)}) while((s32[]{:T(128)}, f32[1,16,64,128]{3,2,1,0:T(8,128)S(1)}, f32[6,1,16,64,128]{4,3,2,1,0:T(8,128)}, ...), condition=%wide.region_7.8_spmd.clone, body=%wide.region_6.7_spmd.clone.sunk | while | flops 524291 | bytes 2622240 | solution.py:82
  102.2 486.0 %while.38 = (s32[]{:T(128)}, f32[1,16,64,128]{3,2,1,0:T(8,128)S(1)}, f32[1,16,1,1]{1,3,2,0:T(1,128)S(1)}, f32[1,16,64,128]{3,2,1,0:T(8,128)S(1)}, s32[]{:T(128)}) while((s32[]{:T(128)}, f32[1,16,64,128]{3,2,1,0:T(8,128)S(1)}, f32[1,16,1,1]{1,3,2,0:T(1,128)S(1)}, f32[1,16,64,128]{3,2,1,0:T(8,128)S(1)}, s32[]{:T(128)}) %tuple.69), condition=%wide.region_9.10_spmd, body=%wide.region_8.9_spmd.sunk | while | flops 262146 | bytes 3670181 | solution.py:89
  105.4 14.2 %collective-permute-done = f32[1,16,64,128]{3,2,1,0:T(8,128)S(1)} collective-permute-done((f32[1,16,64,128]{3,2,1,0:T(8,128)S(1)}, f32[1,16,64,128]{3,2,1,0:T(8,128)S(1)}, u32[]{:S(2)}, u32[]{:S(2)}) %collective-permute-start) | collective-permute-done | bytes 524320 | tf_op jit(solution)/shard_map/while/body/eval_jaxpr/ppermute | solution.py:19
  121.7 14.4 %collective-permute-done = f32[1,16,64,128]{3,2,1,0:T(8,128)S(1)} collective-permute-done((f32[1,16,64,128]{3,2,1,0:T(8,128)S(1)}, f32[1,16,64,128]{3,2,1,0:T(8,128)S(1)}, u32[]{:S(2)}, u32[]{:S(2)}) %collective-permute-start) | collective-permute-done | bytes 524320 | tf_op jit(solution)/shard_map/while/body/eval_jaxpr/ppermute | solution.py:19
  138.2 13.5 %collective-permute-done = f32[1,16,64,128]{3,2,1,0:T(8,128)S(1)} collective-permute-done((f32[1,16,64,128]{3,2,1,0:T(8,128)S(1)}, f32[1,16,64,128]{3,2,1,0:T(8,128)S(1)}, u32[]{:S(2)}, u32[]{:S(2)}) %collective-permute-start) | collective-permute-done | bytes 524320 | tf_op jit(solution)/shard_map/while/body/eval_jaxpr/ppermute | solution.py:19
  153.8 12.6 %collective-permute-done = f32[1,16,64,128]{3,2,1,0:T(8,128)S(1)} collective-permute-done((f32[1,16,64,128]{3,2,1,0:T(8,128)S(1)}, f32[1,16,64,128]{3,2,1,0:T(8,128)S(1)}, u32[]{:S(2)}, u32[]{:S(2)}) %collective-permute-start) | collective-permute-done | bytes 524320 | tf_op jit(solution)/shard_map/while/body/eval_jaxpr/ppermute | solution.py:19
  168.4 11.7 %collective-permute-done = f32[1,16,64,128]{3,2,1,0:T(8,128)S(1)} collective-permute-done((f32[1,16,64,128]{3,2,1,0:T(8,128)S(1)}, f32[1,16,64,128]{3,2,1,0:T(8,128)S(1)}, u32[]{:S(2)}, u32[]{:S(2)}) %collective-permute-start) | collective-permute-done | bytes 524320 | tf_op jit(solution)/shard_map/while/body/eval_jaxpr/ppermute | solution.py:19
  195.5 11.9 %collective-permute-done = f32[1,16,64,128]{3,2,1,0:T(8,128)S(1)} collective-permute-done((f32[1,16,64,128]{3,2,1,0:T(8,128)S(1)}, f32[1,16,64,128]{3,2,1,0:T(8,128)S(1)}, u32[]{:S(2)}, u32[]{:S(2)}) %collective-permute-start) | collective-permute-done | bytes 524320 | tf_op jit(solution)/shard_map/while/body/eval_jaxpr/ppermute | solution.py:19
  209.4 13.0 %collective-permute-done = f32[1,16,64,128]{3,2,1,0:T(8,128)S(1)} collective-permute-done((f32[1,16,64,128]{3,2,1,0:T(8,128)S(1)}, f32[1,16,64,128]{3,2,1,0:T(8,128)S(1)}, u32[]{:S(2)}, u32[]{:S(2)}) %collective-permute-start) | collective-permute-done | bytes 524320 | tf_op jit(solution)/shard_map/while/body/eval_jaxpr/ppermute | solution.py:19
  224.5 14.1 %collective-permute-done = f32[1,16,64,128]{3,2,1,0:T(8,128)S(1)} collective-permute-done((f32[1,16,64,128]{3,2,1,0:T(8,128)S(1)}, f32[1,16,64,128]{3,2,1,0:T(8,128)S(1)}, u32[]{:S(2)}, u32[]{:S(2)}) %collective-permute-start) | collective-permute-done | bytes 524320 | tf_op jit(solution)/shard_map/while/body/eval_jaxpr/ppermute | solution.py:19
  240.6 15.1 %collective-permute-done = f32[1,16,64,128]{3,2,1,0:T(8,128)S(1)} collective-permute-done((f32[1,16,64,128]{3,2,1,0:T(8,128)S(1)}, f32[1,16,64,128]{3,2,1,0:T(8,128)S(1)}, u32[]{:S(2)}, u32[]{:S(2)}) %collective-permute-start) | collective-permute-done | bytes 524320 | tf_op jit(solution)/shard_map/while/body/eval_jaxpr/ppermute | solution.py:19
  257.8 16.4 %collective-permute-done = f32[1,16,64,128]{3,2,1,0:T(8,128)S(1)} collective-permute-done((f32[1,16,64,128]{3,2,1,0:T(8,128)S(1)}, f32[1,16,64,128]{3,2,1,0:T(8,128)S(1)}, u32[]{:S(2)}, u32[]{:S(2)}) %collective-permute-start) | collective-permute-done | bytes 524320 | tf_op jit(solution)/shard_map/while/body/eval_jaxpr/ppermute | solution.py:19
  276.2 16.2 %collective-permute-done = f32[1,16,64,128]{3,2,1,0:T(8,128)S(1)} collective-permute-done((f32[1,16,64,128]{3,2,1,0:T(8,128)S(1)}, f32[1,16,64,128]{3,2,1,0:T(8,128)S(1)}, u32[]{:S(2)}, u32[]{:S(2)}) %collective-permute-start) | collective-permute-done | bytes 524320 | tf_op jit(solution)/shard_map/while/body/eval_jaxpr/ppermute | solution.py:19
  294.5 15.4 %collective-permute-done = f32[1,16,64,128]{3,2,1,0:T(8,128)S(1)} collective-permute-done((f32[1,16,64,128]{3,2,1,0:T(8,128)S(1)}, f32[1,16,64,128]{3,2,1,0:T(8,128)S(1)}, u32[]{:S(2)}, u32[]{:S(2)}) %collective-permute-start) | collective-permute-done | bytes 524320 | tf_op jit(solution)/shard_map/while/body/eval_jaxpr/ppermute | solution.py:19
  312.0 14.5 %collective-permute-done = f32[1,16,64,128]{3,2,1,0:T(8,128)S(1)} collective-permute-done((f32[1,16,64,128]{3,2,1,0:T(8,128)S(1)}, f32[1,16,64,128]{3,2,1,0:T(8,128)S(1)}, u32[]{:S(2)}, u32[]{:S(2)}) %collective-permute-start) | collective-permute-done | bytes 524320 | tf_op jit(solution)/shard_map/while/body/eval_jaxpr/ppermute | solution.py:19
  328.5 13.6 %collective-permute-done = f32[1,16,64,128]{3,2,1,0:T(8,128)S(1)} collective-permute-done((f32[1,16,64,128]{3,2,1,0:T(8,128)S(1)}, f32[1,16,64,128]{3,2,1,0:T(8,128)S(1)}, u32[]{:S(2)}, u32[]{:S(2)}) %collective-permute-start) | collective-permute-done | bytes 524320 | tf_op jit(solution)/shard_map/while/body/eval_jaxpr/ppermute | solution.py:19
  344.2 12.7 %collective-permute-done = f32[1,16,64,128]{3,2,1,0:T(8,128)S(1)} collective-permute-done((f32[1,16,64,128]{3,2,1,0:T(8,128)S(1)}, f32[1,16,64,128]{3,2,1,0:T(8,128)S(1)}, u32[]{:S(2)}, u32[]{:S(2)}) %collective-permute-start) | collective-permute-done | bytes 524320 | tf_op jit(solution)/shard_map/while/body/eval_jaxpr/ppermute | solution.py:19
  358.9 11.8 %collective-permute-done = f32[1,16,64,128]{3,2,1,0:T(8,128)S(1)} collective-permute-done((f32[1,16,64,128]{3,2,1,0:T(8,128)S(1)}, f32[1,16,64,128]{3,2,1,0:T(8,128)S(1)}, u32[]{:S(2)}, u32[]{:S(2)}) %collective-permute-start) | collective-permute-done | bytes 524320 | tf_op jit(solution)/shard_map/while/body/eval_jaxpr/ppermute | solution.py:19
  386.0 11.8 %collective-permute-done = f32[1,16,64,128]{3,2,1,0:T(8,128)S(1)} collective-permute-done((f32[1,16,64,128]{3,2,1,0:T(8,128)S(1)}, f32[1,16,64,128]{3,2,1,0:T(8,128)S(1)}, u32[]{:S(2)}, u32[]{:S(2)}) %collective-permute-start) | collective-permute-done | bytes 524320 | tf_op jit(solution)/shard_map/while/body/eval_jaxpr/ppermute | solution.py:19
  399.9 12.9 %collective-permute-done = f32[1,16,64,128]{3,2,1,0:T(8,128)S(1)} collective-permute-done((f32[1,16,64,128]{3,2,1,0:T(8,128)S(1)}, f32[1,16,64,128]{3,2,1,0:T(8,128)S(1)}, u32[]{:S(2)}, u32[]{:S(2)}) %collective-permute-start) | collective-permute-done | bytes 524320 | tf_op jit(solution)/shard_map/while/body/eval_jaxpr/ppermute | solution.py:19
  414.9 14.0 %collective-permute-done = f32[1,16,64,128]{3,2,1,0:T(8,128)S(1)} collective-permute-done((f32[1,16,64,128]{3,2,1,0:T(8,128)S(1)}, f32[1,16,64,128]{3,2,1,0:T(8,128)S(1)}, u32[]{:S(2)}, u32[]{:S(2)}) %collective-permute-start) | collective-permute-done | bytes 524320 | tf_op jit(solution)/shard_map/while/body/eval_jaxpr/ppermute | solution.py:19
  430.9 15.1 %collective-permute-done = f32[1,16,64,128]{3,2,1,0:T(8,128)S(1)} collective-permute-done((f32[1,16,64,128]{3,2,1,0:T(8,128)S(1)}, f32[1,16,64,128]{3,2,1,0:T(8,128)S(1)}, u32[]{:S(2)}, u32[]{:S(2)}) %collective-permute-start) | collective-permute-done | bytes 524320 | tf_op jit(solution)/shard_map/while/body/eval_jaxpr/ppermute | solution.py:19
  448.1 16.3 %collective-permute-done = f32[1,16,64,128]{3,2,1,0:T(8,128)S(1)} collective-permute-done((f32[1,16,64,128]{3,2,1,0:T(8,128)S(1)}, f32[1,16,64,128]{3,2,1,0:T(8,128)S(1)}, u32[]{:S(2)}, u32[]{:S(2)}) %collective-permute-start) | collective-permute-done | bytes 524320 | tf_op jit(solution)/shard_map/while/body/eval_jaxpr/ppermute | solution.py:19
  466.4 16.3 %collective-permute-done = f32[1,16,64,128]{3,2,1,0:T(8,128)S(1)} collective-permute-done((f32[1,16,64,128]{3,2,1,0:T(8,128)S(1)}, f32[1,16,64,128]{3,2,1,0:T(8,128)S(1)}, u32[]{:S(2)}, u32[]{:S(2)}) %collective-permute-start) | collective-permute-done | bytes 524320 | tf_op jit(solution)/shard_map/while/body/eval_jaxpr/ppermute | solution.py:19
  484.8 15.5 %collective-permute-done = f32[1,16,64,128]{3,2,1,0:T(8,128)S(1)} collective-permute-done((f32[1,16,64,128]{3,2,1,0:T(8,128)S(1)}, f32[1,16,64,128]{3,2,1,0:T(8,128)S(1)}, u32[]{:S(2)}, u32[]{:S(2)}) %collective-permute-start) | collective-permute-done | bytes 524320 | tf_op jit(solution)/shard_map/while/body/eval_jaxpr/ppermute | solution.py:19
  502.4 14.6 %collective-permute-done = f32[1,16,64,128]{3,2,1,0:T(8,128)S(1)} collective-permute-done((f32[1,16,64,128]{3,2,1,0:T(8,128)S(1)}, f32[1,16,64,128]{3,2,1,0:T(8,128)S(1)}, u32[]{:S(2)}, u32[]{:S(2)}) %collective-permute-start) | collective-permute-done | bytes 524320 | tf_op jit(solution)/shard_map/while/body/eval_jaxpr/ppermute | solution.py:19
  519.1 13.7 %collective-permute-done = f32[1,16,64,128]{3,2,1,0:T(8,128)S(1)} collective-permute-done((f32[1,16,64,128]{3,2,1,0:T(8,128)S(1)}, f32[1,16,64,128]{3,2,1,0:T(8,128)S(1)}, u32[]{:S(2)}, u32[]{:S(2)}) %collective-permute-start) | collective-permute-done | bytes 524320 | tf_op jit(solution)/shard_map/while/body/eval_jaxpr/ppermute | solution.py:19
  534.8 12.8 %collective-permute-done = f32[1,16,64,128]{3,2,1,0:T(8,128)S(1)} collective-permute-done((f32[1,16,64,128]{3,2,1,0:T(8,128)S(1)}, f32[1,16,64,128]{3,2,1,0:T(8,128)S(1)}, u32[]{:S(2)}, u32[]{:S(2)}) %collective-permute-start) | collective-permute-done | bytes 524320 | tf_op jit(solution)/shard_map/while/body/eval_jaxpr/ppermute | solution.py:19
  549.7 11.9 %collective-permute-done = f32[1,16,64,128]{3,2,1,0:T(8,128)S(1)} collective-permute-done((f32[1,16,64,128]{3,2,1,0:T(8,128)S(1)}, f32[1,16,64,128]{3,2,1,0:T(8,128)S(1)}, u32[]{:S(2)}, u32[]{:S(2)}) %collective-permute-start) | collective-permute-done | bytes 524320 | tf_op jit(solution)/shard_map/while/body/eval_jaxpr/ppermute | solution.py:19
  576.9 11.3 %collective-permute-done = f32[1,16,64,128]{3,2,1,0:T(8,128)S(1)} collective-permute-done((f32[1,16,64,128]{3,2,1,0:T(8,128)S(1)}, f32[1,16,64,128]{3,2,1,0:T(8,128)S(1)}, u32[]{:S(2)}, u32[]{:S(2)}) %collective-permute-start) | collective-permute-done | bytes 524320 | tf_op jit(solution)/shard_map/while/body/eval_jaxpr/ppermute | solution.py:19
  614.3 43.2 %all_to_all.16 = bf16[8,192,1024]{2,1,0:T(8,128)(2,1)S(1)} all-to-all(bf16[8,192,1024]{2,1,0:T(8,128)(2,1)S(1)} %bitcast.182), channel_id=1, replica_groups=mesh['ctx'=32,'head'=8] {'head'}, dimensions={0} | all-to-all | bytes 6291456 | tf_op jit(solution)/shard_map/all_to_all | solution.py:106
  (269 shorter events, 227.4 us)
Async XLA Ops:
  4.4 9.7 %collective-permute-start.1 = (bf16[3,1280]{1,0:T(4,128)(2,1)S(1)}, bf16[3,1280]{1,0:T(4,128)(2,1)S(1)}, u32[]{:S(2)}, u32[]{:S(2)}) collective-permute-start(bf16[3,1280]{1,0:T(4,128)(2,1)S(1)} %slice.72), channel_id=1, source_target_pairs={{0,8},{8,16},{16,24},{24,32},{32,40},{40,48},{48,56},{56,64},{64,7... | collective-permute-start | bytes 23048 | tf_op jit(solution)/shard_map/ppermute | solution.py:19
  102.3 17.3 %collective-permute-start = (f32[1,16,64,128]{3,2,1,0:T(8,128)S(1)}, f32[1,16,64,128]{3,2,1,0:T(8,128)S(1)}, u32[]{:S(2)}, u32[]{:S(2)}) collective-permute-start(f32[1,16,64,128]{3,2,1,0:T(8,128)S(1)} %multiply_add_fusion.2), channel_id=1, source_target_pairs={{0,8},{8,16},{16,24},{24,32},{32,40},{40,48},{48,56},{56,64},{64,7... | collective-permute-start | bytes 1572872 | tf_op jit(solution)/shard_map/while/body/eval_jaxpr/ppermute | solution.py:19
  119.8 16.4 %collective-permute-start = (f32[1,16,64,128]{3,2,1,0:T(8,128)S(1)}, f32[1,16,64,128]{3,2,1,0:T(8,128)S(1)}, u32[]{:S(2)}, u32[]{:S(2)}) collective-permute-start(f32[1,16,64,128]{3,2,1,0:T(8,128)S(1)} %multiply_add_fusion.2), channel_id=1, source_target_pairs={{0,8},{8,16},{16,24},{24,32},{32,40},{40,48},{48,56},{56,64},{64,7... | collective-permute-start | bytes 1572872 | tf_op jit(solution)/shard_map/while/body/eval_jaxpr/ppermute | solution.py:19
  136.3 15.5 %collective-permute-start = (f32[1,16,64,128]{3,2,1,0:T(8,128)S(1)}, f32[1,16,64,128]{3,2,1,0:T(8,128)S(1)}, u32[]{:S(2)}, u32[]{:S(2)}) collective-permute-start(f32[1,16,64,128]{3,2,1,0:T(8,128)S(1)} %multiply_add_fusion.2), channel_id=1, source_target_pairs={{0,8},{8,16},{16,24},{24,32},{32,40},{40,48},{48,56},{56,64},{64,7... | collective-permute-start | bytes 1572872 | tf_op jit(solution)/shard_map/while/body/eval_jaxpr/ppermute | solution.py:19
  151.8 14.5 %collective-permute-start = (f32[1,16,64,128]{3,2,1,0:T(8,128)S(1)}, f32[1,16,64,128]{3,2,1,0:T(8,128)S(1)}, u32[]{:S(2)}, u32[]{:S(2)}) collective-permute-start(f32[1,16,64,128]{3,2,1,0:T(8,128)S(1)} %multiply_add_fusion.2), channel_id=1, source_target_pairs={{0,8},{8,16},{16,24},{24,32},{32,40},{40,48},{48,56},{56,64},{64,7... | collective-permute-start | bytes 1572872 | tf_op jit(solution)/shard_map/while/body/eval_jaxpr/ppermute | solution.py:19
  166.5 13.6 %collective-permute-start = (f32[1,16,64,128]{3,2,1,0:T(8,128)S(1)}, f32[1,16,64,128]{3,2,1,0:T(8,128)S(1)}, u32[]{:S(2)}, u32[]{:S(2)}) collective-permute-start(f32[1,16,64,128]{3,2,1,0:T(8,128)S(1)} %multiply_add_fusion.2), channel_id=1, source_target_pairs={{0,8},{8,16},{16,24},{24,32},{32,40},{40,48},{48,56},{56,64},{64,7... | collective-permute-start | bytes 1572872 | tf_op jit(solution)/shard_map/while/body/eval_jaxpr/ppermute | solution.py:19
  180.2 13.2 %collective-permute-start = (f32[1,16,64,128]{3,2,1,0:T(8,128)S(1)}, f32[1,16,64,128]{3,2,1,0:T(8,128)S(1)}, u32[]{:S(2)}, u32[]{:S(2)}) collective-permute-start(f32[1,16,64,128]{3,2,1,0:T(8,128)S(1)} %multiply_add_fusion.2), channel_id=1, source_target_pairs={{0,8},{8,16},{16,24},{24,32},{32,40},{40,48},{48,56},{56,64},{64,7... | collective-permute-start | bytes 1572872 | tf_op jit(solution)/shard_map/while/body/eval_jaxpr/ppermute | solution.py:19
  193.5 13.8 %collective-permute-start = (f32[1,16,64,128]{3,2,1,0:T(8,128)S(1)}, f32[1,16,64,128]{3,2,1,0:T(8,128)S(1)}, u32[]{:S(2)}, u32[]{:S(2)}) collective-permute-start(f32[1,16,64,128]{3,2,1,0:T(8,128)S(1)} %multiply_add_fusion.2), channel_id=1, source_target_pairs={{0,8},{8,16},{16,24},{24,32},{32,40},{40,48},{48,56},{56,64},{64,7... | collective-permute-start | bytes 1572872 | tf_op jit(solution)/shard_map/while/body/eval_jaxpr/ppermute | solution.py:19
  207.5 14.9 %collective-permute-start = (f32[1,16,64,128]{3,2,1,0:T(8,128)S(1)}, f32[1,16,64,128]{3,2,1,0:T(8,128)S(1)}, u32[]{:S(2)}, u32[]{:S(2)}) collective-permute-start(f32[1,16,64,128]{3,2,1,0:T(8,128)S(1)} %multiply_add_fusion.2), channel_id=1, source_target_pairs={{0,8},{8,16},{16,24},{24,32},{32,40},{40,48},{48,56},{56,64},{64,7... | collective-permute-start | bytes 1572872 | tf_op jit(solution)/shard_map/while/body/eval_jaxpr/ppermute | solution.py:19
  222.5 16.0 %collective-permute-start = (f32[1,16,64,128]{3,2,1,0:T(8,128)S(1)}, f32[1,16,64,128]{3,2,1,0:T(8,128)S(1)}, u32[]{:S(2)}, u32[]{:S(2)}) collective-permute-start(f32[1,16,64,128]{3,2,1,0:T(8,128)S(1)} %multiply_add_fusion.2), channel_id=1, source_target_pairs={{0,8},{8,16},{16,24},{24,32},{32,40},{40,48},{48,56},{56,64},{64,7... | collective-permute-start | bytes 1572872 | tf_op jit(solution)/shard_map/while/body/eval_jaxpr/ppermute | solution.py:19
  238.7 17.1 %collective-permute-start = (f32[1,16,64,128]{3,2,1,0:T(8,128)S(1)}, f32[1,16,64,128]{3,2,1,0:T(8,128)S(1)}, u32[]{:S(2)}, u32[]{:S(2)}) collective-permute-start(f32[1,16,64,128]{3,2,1,0:T(8,128)S(1)} %multiply_add_fusion.2), channel_id=1, source_target_pairs={{0,8},{8,16},{16,24},{24,32},{32,40},{40,48},{48,56},{56,64},{64,7... | collective-permute-start | bytes 1572872 | tf_op jit(solution)/shard_map/while/body/eval_jaxpr/ppermute | solution.py:19
  255.9 18.3 %collective-permute-start = (f32[1,16,64,128]{3,2,1,0:T(8,128)S(1)}, f32[1,16,64,128]{3,2,1,0:T(8,128)S(1)}, u32[]{:S(2)}, u32[]{:S(2)}) collective-permute-start(f32[1,16,64,128]{3,2,1,0:T(8,128)S(1)} %multiply_add_fusion.2), channel_id=1, source_target_pairs={{0,8},{8,16},{16,24},{24,32},{32,40},{40,48},{48,56},{56,64},{64,7... | collective-permute-start | bytes 1572872 | tf_op jit(solution)/shard_map/while/body/eval_jaxpr/ppermute | solution.py:19
  274.3 18.2 %collective-permute-start = (f32[1,16,64,128]{3,2,1,0:T(8,128)S(1)}, f32[1,16,64,128]{3,2,1,0:T(8,128)S(1)}, u32[]{:S(2)}, u32[]{:S(2)}) collective-permute-start(f32[1,16,64,128]{3,2,1,0:T(8,128)S(1)} %multiply_add_fusion.2), channel_id=1, source_target_pairs={{0,8},{8,16},{16,24},{24,32},{32,40},{40,48},{48,56},{56,64},{64,7... | collective-permute-start | bytes 1572872 | tf_op jit(solution)/shard_map/while/body/eval_jaxpr/ppermute | solution.py:19
  292.6 17.4 %collective-permute-start = (f32[1,16,64,128]{3,2,1,0:T(8,128)S(1)}, f32[1,16,64,128]{3,2,1,0:T(8,128)S(1)}, u32[]{:S(2)}, u32[]{:S(2)}) collective-permute-start(f32[1,16,64,128]{3,2,1,0:T(8,128)S(1)} %multiply_add_fusion.2), channel_id=1, source_target_pairs={{0,8},{8,16},{16,24},{24,32},{32,40},{40,48},{48,56},{56,64},{64,7... | collective-permute-start | bytes 1572872 | tf_op jit(solution)/shard_map/while/body/eval_jaxpr/ppermute | solution.py:19
  310.0 16.4 %collective-permute-start = (f32[1,16,64,128]{3,2,1,0:T(8,128)S(1)}, f32[1,16,64,128]{3,2,1,0:T(8,128)S(1)}, u32[]{:S(2)}, u32[]{:S(2)}) collective-permute-start(f32[1,16,64,128]{3,2,1,0:T(8,128)S(1)} %multiply_add_fusion.2), channel_id=1, source_target_pairs={{0,8},{8,16},{16,24},{24,32},{32,40},{40,48},{48,56},{56,64},{64,7... | collective-permute-start | bytes 1572872 | tf_op jit(solution)/shard_map/while/body/eval_jaxpr/ppermute | solution.py:19
  326.6 15.5 %collective-permute-start = (f32[1,16,64,128]{3,2,1,0:T(8,128)S(1)}, f32[1,16,64,128]{3,2,1,0:T(8,128)S(1)}, u32[]{:S(2)}, u32[]{:S(2)}) collective-permute-start(f32[1,16,64,128]{3,2,1,0:T(8,128)S(1)} %multiply_add_fusion.2), channel_id=1, source_target_pairs={{0,8},{8,16},{16,24},{24,32},{32,40},{40,48},{48,56},{56,64},{64,7... | collective-permute-start | bytes 1572872 | tf_op jit(solution)/shard_map/while/body/eval_jaxpr/ppermute | solution.py:19
  342.3 14.6 %collective-permute-start = (f32[1,16,64,128]{3,2,1,0:T(8,128)S(1)}, f32[1,16,64,128]{3,2,1,0:T(8,128)S(1)}, u32[]{:S(2)}, u32[]{:S(2)}) collective-permute-start(f32[1,16,64,128]{3,2,1,0:T(8,128)S(1)} %multiply_add_fusion.2), channel_id=1, source_target_pairs={{0,8},{8,16},{16,24},{24,32},{32,40},{40,48},{48,56},{56,64},{64,7... | collective-permute-start | bytes 1572872 | tf_op jit(solution)/shard_map/while/body/eval_jaxpr/ppermute | solution.py:19
  357.0 13.7 %collective-permute-start = (f32[1,16,64,128]{3,2,1,0:T(8,128)S(1)}, f32[1,16,64,128]{3,2,1,0:T(8,128)S(1)}, u32[]{:S(2)}, u32[]{:S(2)}) collective-permute-start(f32[1,16,64,128]{3,2,1,0:T(8,128)S(1)} %multiply_add_fusion.2), channel_id=1, source_target_pairs={{0,8},{8,16},{16,24},{24,32},{32,40},{40,48},{48,56},{56,64},{64,7... | collective-permute-start | bytes 1572872 | tf_op jit(solution)/shard_map/while/body/eval_jaxpr/ppermute | solution.py:19
  370.8 13.2 %collective-permute-start = (f32[1,16,64,128]{3,2,1,0:T(8,128)S(1)}, f32[1,16,64,128]{3,2,1,0:T(8,128)S(1)}, u32[]{:S(2)}, u32[]{:S(2)}) collective-permute-start(f32[1,16,64,128]{3,2,1,0:T(8,128)S(1)} %multiply_add_fusion.2), channel_id=1, source_target_pairs={{0,8},{8,16},{16,24},{24,32},{32,40},{40,48},{48,56},{56,64},{64,7... | collective-permute-start | bytes 1572872 | tf_op jit(solution)/shard_map/while/body/eval_jaxpr/ppermute | solution.py:19
  384.1 13.8 %collective-permute-start = (f32[1,16,64,128]{3,2,1,0:T(8,128)S(1)}, f32[1,16,64,128]{3,2,1,0:T(8,128)S(1)}, u32[]{:S(2)}, u32[]{:S(2)}) collective-permute-start(f32[1,16,64,128]{3,2,1,0:T(8,128)S(1)} %multiply_add_fusion.2), channel_id=1, source_target_pairs={{0,8},{8,16},{16,24},{24,32},{32,40},{40,48},{48,56},{56,64},{64,7... | collective-permute-start | bytes 1572872 | tf_op jit(solution)/shard_map/while/body/eval_jaxpr/ppermute | solution.py:19
  398.0 14.8 %collective-permute-start = (f32[1,16,64,128]{3,2,1,0:T(8,128)S(1)}, f32[1,16,64,128]{3,2,1,0:T(8,128)S(1)}, u32[]{:S(2)}, u32[]{:S(2)}) collective-permute-start(f32[1,16,64,128]{3,2,1,0:T(8,128)S(1)} %multiply_add_fusion.2), channel_id=1, source_target_pairs={{0,8},{8,16},{16,24},{24,32},{32,40},{40,48},{48,56},{56,64},{64,7... | collective-permute-start | bytes 1572872 | tf_op jit(solution)/shard_map/while/body/eval_jaxpr/ppermute | solution.py:19
  412.9 15.9 %collective-permute-start = (f32[1,16,64,128]{3,2,1,0:T(8,128)S(1)}, f32[1,16,64,128]{3,2,1,0:T(8,128)S(1)}, u32[]{:S(2)}, u32[]{:S(2)}) collective-permute-start(f32[1,16,64,128]{3,2,1,0:T(8,128)S(1)} %multiply_add_fusion.2), channel_id=1, source_target_pairs={{0,8},{8,16},{16,24},{24,32},{32,40},{40,48},{48,56},{56,64},{64,7... | collective-permute-start | bytes 1572872 | tf_op jit(solution)/shard_map/while/body/eval_jaxpr/ppermute | solution.py:19
  429.0 17.0 %collective-permute-start = (f32[1,16,64,128]{3,2,1,0:T(8,128)S(1)}, f32[1,16,64,128]{3,2,1,0:T(8,128)S(1)}, u32[]{:S(2)}, u32[]{:S(2)}) collective-permute-start(f32[1,16,64,128]{3,2,1,0:T(8,128)S(1)} %multiply_add_fusion.2), channel_id=1, source_target_pairs={{0,8},{8,16},{16,24},{24,32},{32,40},{40,48},{48,56},{56,64},{64,7... | collective-permute-start | bytes 1572872 | tf_op jit(solution)/shard_map/while/body/eval_jaxpr/ppermute | solution.py:19
  446.1 18.2 %collective-permute-start = (f32[1,16,64,128]{3,2,1,0:T(8,128)S(1)}, f32[1,16,64,128]{3,2,1,0:T(8,128)S(1)}, u32[]{:S(2)}, u32[]{:S(2)}) collective-permute-start(f32[1,16,64,128]{3,2,1,0:T(8,128)S(1)} %multiply_add_fusion.2), channel_id=1, source_target_pairs={{0,8},{8,16},{16,24},{24,32},{32,40},{40,48},{48,56},{56,64},{64,7... | collective-permute-start | bytes 1572872 | tf_op jit(solution)/shard_map/while/body/eval_jaxpr/ppermute | solution.py:19
  464.5 18.3 %collective-permute-start = (f32[1,16,64,128]{3,2,1,0:T(8,128)S(1)}, f32[1,16,64,128]{3,2,1,0:T(8,128)S(1)}, u32[]{:S(2)}, u32[]{:S(2)}) collective-permute-start(f32[1,16,64,128]{3,2,1,0:T(8,128)S(1)} %multiply_add_fusion.2), channel_id=1, source_target_pairs={{0,8},{8,16},{16,24},{24,32},{32,40},{40,48},{48,56},{56,64},{64,7... | collective-permute-start | bytes 1572872 | tf_op jit(solution)/shard_map/while/body/eval_jaxpr/ppermute | solution.py:19
  482.8 17.5 %collective-permute-start = (f32[1,16,64,128]{3,2,1,0:T(8,128)S(1)}, f32[1,16,64,128]{3,2,1,0:T(8,128)S(1)}, u32[]{:S(2)}, u32[]{:S(2)}) collective-permute-start(f32[1,16,64,128]{3,2,1,0:T(8,128)S(1)} %multiply_add_fusion.2), channel_id=1, source_target_pairs={{0,8},{8,16},{16,24},{24,32},{32,40},{40,48},{48,56},{56,64},{64,7... | collective-permute-start | bytes 1572872 | tf_op jit(solution)/shard_map/while/body/eval_jaxpr/ppermute | solution.py:19
  500.4 16.6 %collective-permute-start = (f32[1,16,64,128]{3,2,1,0:T(8,128)S(1)}, f32[1,16,64,128]{3,2,1,0:T(8,128)S(1)}, u32[]{:S(2)}, u32[]{:S(2)}) collective-permute-start(f32[1,16,64,128]{3,2,1,0:T(8,128)S(1)} %multiply_add_fusion.2), channel_id=1, source_target_pairs={{0,8},{8,16},{16,24},{24,32},{32,40},{40,48},{48,56},{56,64},{64,7... | collective-permute-start | bytes 1572872 | tf_op jit(solution)/shard_map/while/body/eval_jaxpr/ppermute | solution.py:19
  517.1 15.7 %collective-permute-start = (f32[1,16,64,128]{3,2,1,0:T(8,128)S(1)}, f32[1,16,64,128]{3,2,1,0:T(8,128)S(1)}, u32[]{:S(2)}, u32[]{:S(2)}) collective-permute-start(f32[1,16,64,128]{3,2,1,0:T(8,128)S(1)} %multiply_add_fusion.2), channel_id=1, source_target_pairs={{0,8},{8,16},{16,24},{24,32},{32,40},{40,48},{48,56},{56,64},{64,7... | collective-permute-start | bytes 1572872 | tf_op jit(solution)/shard_map/while/body/eval_jaxpr/ppermute | solution.py:19
  532.9 14.7 %collective-permute-start = (f32[1,16,64,128]{3,2,1,0:T(8,128)S(1)}, f32[1,16,64,128]{3,2,1,0:T(8,128)S(1)}, u32[]{:S(2)}, u32[]{:S(2)}) collective-permute-start(f32[1,16,64,128]{3,2,1,0:T(8,128)S(1)} %multiply_add_fusion.2), channel_id=1, source_target_pairs={{0,8},{8,16},{16,24},{24,32},{32,40},{40,48},{48,56},{56,64},{64,7... | collective-permute-start | bytes 1572872 | tf_op jit(solution)/shard_map/while/body/eval_jaxpr/ppermute | solution.py:19
  547.8 13.8 %collective-permute-start = (f32[1,16,64,128]{3,2,1,0:T(8,128)S(1)}, f32[1,16,64,128]{3,2,1,0:T(8,128)S(1)}, u32[]{:S(2)}, u32[]{:S(2)}) collective-permute-start(f32[1,16,64,128]{3,2,1,0:T(8,128)S(1)} %multiply_add_fusion.2), channel_id=1, source_target_pairs={{0,8},{8,16},{16,24},{24,32},{32,40},{40,48},{48,56},{56,64},{64,7... | collective-permute-start | bytes 1572872 | tf_op jit(solution)/shard_map/while/body/eval_jaxpr/ppermute | solution.py:19
  561.7 13.2 %collective-permute-start = (f32[1,16,64,128]{3,2,1,0:T(8,128)S(1)}, f32[1,16,64,128]{3,2,1,0:T(8,128)S(1)}, u32[]{:S(2)}, u32[]{:S(2)}) collective-permute-start(f32[1,16,64,128]{3,2,1,0:T(8,128)S(1)} %multiply_add_fusion.2), channel_id=1, source_target_pairs={{0,8},{8,16},{16,24},{24,32},{32,40},{40,48},{48,56},{56,64},{64,7... | collective-permute-start | bytes 1572872 | tf_op jit(solution)/shard_map/while/body/eval_jaxpr/ppermute | solution.py:19
  575.0 13.2 %collective-permute-start = (f32[1,16,64,128]{3,2,1,0:T(8,128)S(1)}, f32[1,16,64,128]{3,2,1,0:T(8,128)S(1)}, u32[]{:S(2)}, u32[]{:S(2)}) collective-permute-start(f32[1,16,64,128]{3,2,1,0:T(8,128)S(1)} %multiply_add_fusion.2), channel_id=1, source_target_pairs={{0,8},{8,16},{16,24},{24,32},{32,40},{40,48},{48,56},{56,64},{64,7... | collective-permute-start | bytes 1572872 | tf_op jit(solution)/shard_map/while/body/eval_jaxpr/ppermute | solution.py:19
  (9 other events, 528.8 us)
where the time goes:
time: 662 us; the launch traced here: 660 us
  waiting for transfers between devices  422 us (64%)
  starting transfers between devices  64.5 us (10%)
  local copies, waits for them, and re-layouts  50.5 us (8%)
  blocking collectives  43.2 us (7%)
  matrix products  43 us (6%)
  other arithmetic  34.8 us (5%)
    ppermute x32, waiting for transfers between devices, passed_along(): return lax.ppermute(value, axis, pairs)  422 us
    ppermute x32, starting transfers between devices, passed_along(): return lax.ppermute(value, axis, pairs)  64.5 us
    all_to_all x1, blocking collectives, per_device(): lax.all_to_all(normed, 'head', split_axis=0, concat_axis=1, tiled=True)  43.2 us
    dot_general x6, matrix products, stretch_terms(): jnp.einsum('tsgh,sghp->tghp', weights, values, preferred_element_type=jnp...  20.5 us
  transfers between devices with their start and end apart: 32, of which 32 were waited for; matrix products, arithmetic and copies ran while one was open for 1% of the time, Pallas kernels for 0%

commit v1 on v0

v1 whole, which is shorter than its diff:
```python
import jax
import jax.numpy as jnp
from jax import lax
from jax.experimental import pallas as pl
from jax.experimental.pallas import tpu as pltpu
from jax.sharding import PartitionSpec as P

HEAD_DIM = 64
STATE = 128
TAPS = 4
EPSILON = 1e-05
HI = lax.Precision.HIGHEST
MESH = pl.DeviceIdType.MESH
F32 = jnp.float32
BF16 = jnp.bfloat16

ROWS = 1536
COLS = 1024
HEADS = 16
BLOCK = 128
BLOCKS = ROWS // BLOCK
PARTS = 4
WIDE = COLS // PARTS
ZS = 8
XS = 4
SLICE = STATE // ZS
LEAD = 16
SUB = 64


def iota(shape, dim):
    return lax.broadcasted_iota(jnp.int32, shape, dim)


def dot(a, b, precision=None):
    return jnp.dot(a, b, precision=precision, preferred_element_type=F32)


def silu(v):
    half = 0.5 * v
    return half + half * jnp.tanh(half)


def split_in_two(v):
    high = v.astype(BF16)
    return high, (v - high.astype(F32)).astype(BF16)


def kernel(
    ch_hbm, bc_hbm, gate_hbm, step_hbm, taps, map_taps, rates, skip, gain, out,
    ch, bc, gate, step, wide, xs, bs, bt, cs, cum_v, step_v, tails, decays, spread,
    rows_v, skip_v, state, entering, y0, staged, gated_v,
    zs, z1, prefix, xt, x1, back, incoming, dl, dl_in, tl, tl_in, za, xa,
    in_sem, halo_s, halo_r, dl_s, dl_r, tl_s, tl_r, z1_s, z1_r, x1_s, x1_r, z2_s, z2_r,
    y_s, y_r, own_sem,
):
    c = lax.axis_index("ctx")
    me = lax.axis_index("head")
    x, z = c // ZS, c % ZS
    y, core = me // 2, me % 2

    loads = [pltpu.make_async_copy(step_hbm, step, in_sem.at[0])]
    loads.append(pltpu.make_async_copy(bc_hbm, bc.at[pl.ds(LEAD, ROWS)], in_sem.at[1]))
    for q in range(PARTS):
        part = pl.ds(q * WIDE, WIDE)
        loads.append(
            pltpu.make_async_copy(
                ch_hbm.at[:, part], ch.at[pl.ds(LEAD, ROWS), part], in_sem.at[2 + q]
            )
        )
    loads.append(pltpu.make_async_copy(gate_hbm, gate, in_sem.at[2 + PARTS]))
    for load in loads:
        load.start()

    def z_peer(d):
        return (x * ZS + (z + d) % ZS, me)

    def x_peer(d):
        return (((x + d) % XS) * ZS + z, me)

    after, before = ((c + 1) % (XS * ZS), me), ((c + XS * ZS - 1) % (XS * ZS), me)
    peers = [z_peer(d) for d in range(1, ZS)] + [x_peer(d) for d in range(1, XS)]
    peers += [(c, (me + d) % 8) for d in range(1, 8)] + [after, before]
    barrier = pltpu.get_barrier_semaphore()
    for peer in peers:
        pl.semaphore_signal(barrier, inc=1, device_id=peer, device_id_type=MESH)

    spread[...] = (iota((2 * HEADS, COLS), 0) % HEADS == iota((2 * HEADS, COLS), 1) // HEAD_DIM).astype(BF16)
    head_of = (iota((HEADS, COLS), 0) == iota((HEADS, COLS), 1) // HEAD_DIM).astype(F32)
    loads[0].wait()
    bias = rates[0:1, :]
    raw = jnp.concatenate(
        [(step[pl.ds(k * BLOCK, BLOCK), :] + bias).T for k in range(BLOCKS)], 0
    )
    rate = jnp.broadcast_to(jnp.exp(rates[1:2, :]), (BLOCK, HEADS)).T
    rate = jnp.concatenate([rate] * BLOCKS, 0)
    sizes = jnp.maximum(raw, 0.0) + jnp.log1p(jnp.exp(-jnp.abs(raw)))
    logs = -rate * sizes
    row, col = iota((BLOCK, BLOCK), 0), iota((BLOCK, BLOCK), 1)
    cum = dot(logs, (row <= col).astype(F32), HI)
    rest = dot(logs, (row > col).astype(F32), HI)
    cum_v[...] = cum
    step_v[...] = sizes
    for source, held in ((jnp.exp(rest) * sizes, tails), (jnp.exp(cum), decays)):
        high, low = split_in_two(source)
        for k in range(BLOCKS):
            held[k, 0:HEADS, :] = high[k * HEADS : (k + 1) * HEADS]
            held[k, HEADS : 2 * HEADS, :] = low[k * HEADS : (k + 1) * HEADS]
    count = BLOCKS * HEADS
    own_head = (iota((count, HEADS), 0) % HEADS == iota((count, HEADS), 1)).astype(F32)
    own_block = (iota((16, count), 0) == iota((16, count), 1) // HEADS).astype(F32)
    totals = dot(own_block, cum[:, BLOCK - 1 : BLOCK] * own_head, HI)
    earlier = dot((iota((16, 16), 0) > iota((16, 16), 1)).astype(F32), totals, HI)
    rows_v[...] = jnp.exp(dot(jnp.concatenate([totals, earlier], 0), head_of, HI))
    skip_v[...] = dot(jnp.broadcast_to(skip[...], (8, HEADS)), head_of, HI)
    whole = jnp.broadcast_to(earlier[BLOCKS : BLOCKS + 1], (8, HEADS))
    dl[...] = dot(whole, (iota((HEADS, 128), 0) == iota((HEADS, 128), 1)).astype(F32), HI)

    pl.semaphore_wait(barrier, len(peers))
    halo = [
        pltpu.make_async_remote_copy(
            src_ref=source.at[pl.ds(ROWS - LEAD, LEAD)], dst_ref=held.at[pl.ds(0, LEAD)],
            send_sem=halo_s.at[i], recv_sem=halo_r.at[i], device_id=after, device_id_type=MESH,
        )
        for i, (source, held) in enumerate(((bc_hbm, bc), (ch_hbm, ch)))
    ]
    for copy in halo:
        copy.start()
    dl_in[z] = dl[...]
    dl_copies = [
        pltpu.make_async_remote_copy(
            src_ref=dl, dst_ref=dl_in.at[z], send_sem=dl_s.at[d], recv_sem=dl_r.at[d],
            device_id=z_peer(d), device_id_type=MESH,
        )
        for d in range(1, ZS)
    ]
    for copy in dl_copies:
        copy.start()

    def conv(held, k, lane, weights):
        start = pl.multiple_of(k * BLOCK, BLOCK)
        block = held[pl.ds(start, BLOCK + LEAD), pl.ds(lane, 128)].astype(F32)
        wide[...] = block
        total = weights[0:1, pl.ds(lane, 128)] * wide[pl.ds(LEAD - 3, BLOCK), :]
        for tap in range(1, TAPS):
            total += weights[tap : tap + 1, pl.ds(lane, 128)] * wide[pl.ds(LEAD - 3 + tap, BLOCK), :]
        return silu(total)

    def maps(k):
        start = pl.multiple_of(k * BLOCK, BLOCK)
        b = conv(bc, k, 0, map_taps)
        bs[pl.ds(start, BLOCK), :] = b.astype(BF16)
        bt[k] = b.T.astype(BF16)
        cs[pl.ds(start, BLOCK), :] = conv(bc, k, STATE, map_taps).astype(BF16)

    loads[1].wait()

    @pl.loop(1, BLOCKS)
    def _(k):
        maps(k)

    for load in loads[2 : 2 + PARTS]:
        load.wait()
    for copy in halo:
        copy.wait()

    @pl.when(c == 0)
    def _():
        bc[pl.ds(0, LEAD), :] = jnp.zeros((LEAD, 2 * STATE), BF16)
        ch[pl.ds(0, LEAD), :] = jnp.zeros((LEAD, COLS), BF16)

    maps(0)

    def local_states(q):
        part = pl.ds(q * WIDE, WIDE)
        state[...] = jnp.zeros((STATE, WIDE), F32)

        @pl.loop(0, BLOCKS)
        def _(k):
            start = pl.multiple_of(k * BLOCK, BLOCK)
            entering[k, :, part] = state[...].astype(BF16)
            weights = lax.dot_general(
                tails[k], spread[:, part], (((0,), (0,)), ((), ())), preferred_element_type=F32
            )
            tail = []
            for i in range(WIDE // 128):
                lane = q * WIDE + i * 128
                value = conv(ch, k, lane, taps).astype(BF16)
                xs[pl.ds(start, BLOCK), pl.ds(lane, 128)] = value
                tail.append((value.astype(F32) * weights[:, i * 128 : (i + 1) * 128]).astype(BF16))
            summary = dot(bt[k], jnp.concatenate(tail, 1))
            state[...] = rows_v[pl.ds(k, 1), part] * state[...] + summary

        zs[q] = state[...].astype(BF16)
        mine = pl.ds(pl.multiple_of(z * SLICE, SLICE), SLICE)
        z1[q, z] = state[mine, :].astype(BF16)
        copies = []
        for d in range(1, ZS):
            there = pl.ds(pl.multiple_of(((z + d) % ZS) * SLICE, SLICE), SLICE)
            copies.append(
                pltpu.make_async_remote_copy(
                    src_ref=zs.at[q, there], dst_ref=z1.at[q, z], send_sem=z1_s.at[q, d],
                    recv_sem=z1_r.at[q, d], device_id=z_peer(d), device_id_type=MESH,
                )
            )
        for copy in copies:
            copy.start()
        return copies

    def shard_decays():
        for copy in dl_copies:
            copy.wait()
        each = jnp.concatenate([dl_in[i, 0:1, :] for i in range(ZS)], 0)
        ahead = dot((iota((ZS, ZS), 0) > iota((ZS, ZS), 1)).astype(F32), each, HI)
        both = jnp.concatenate([each, ahead], 0)
        za[...] = jnp.exp(dot(both[:, :HEADS], head_of, HI))
        tl[...] = jnp.broadcast_to(jnp.sum(each, 0, keepdims=True), (8, 128))
        tl_in[x] = tl[...]
        copies = [
            pltpu.make_async_remote_copy(
                src_ref=tl, dst_ref=tl_in.at[x], send_sem=tl_s.at[d], recv_sem=tl_r.at[d],
                device_id=x_peer(d), device_id_type=MESH,
            )
            for d in range(1, XS)
        ]
        for copy in copies:
            copy.start()
        return copies

    def ring_decays(copies):
        for copy in copies:
            copy.wait()
        each = jnp.concatenate([tl_in[i, 0:1, :] for i in range(XS)] * 2, 0)
        xa[...] = jnp.exp(dot(each[:, :HEADS], head_of, HI))

    def along_z(q, copies):
        part = pl.ds(q * WIDE, WIDE)
        for copy in copies:
            copy.wait()
        total = jnp.zeros((SLICE, WIDE), F32)
        for i in range(ZS):
            prefix[q, i] = total
            total = za[i : i + 1, part] * total + z1[q, i].astype(F32)
        own = total.astype(BF16)
        xt[q] = own
        x1[q, x] = own
        copies = [
            pltpu.make_async_remote_copy(
                src_ref=xt.at[q], dst_ref=x1.at[q, x], send_sem=x1_s.at[q, d],
                recv_sem=x1_r.at[q, d], device_id=x_peer(d), device_id_type=MESH,
            )
            for d in range(1, XS)
        ]
        for copy in copies:
            copy.start()
        return copies

    def along_x(q, copies):
        part = pl.ds(q * WIDE, WIDE)
        for copy in copies:
            copy.wait()
        total = jnp.zeros((SLICE, WIDE), F32)
        for i in range(XS - 1):
            total = jnp.where(i < x, xa[i : i + 1, part] * total + x1[q, i].astype(F32), total)
        for i in range(ZS):
            back[q, i] = (prefix[q, i] + za[ZS + i : ZS + i + 1, part] * total).astype(BF16)
        mine = pl.ds(pl.multiple_of(z * SLICE, SLICE), SLICE)
        incoming[q, mine, :] = back[q, z]
        copies = [
            pltpu.make_async_remote_copy(
                src_ref=back.at[q, (z + d) % ZS], dst_ref=incoming.at[q, mine], send_sem=z2_s.at[q, d],
                recv_sem=z2_r.at[q, d], device_id=z_peer(d), device_id_type=MESH,
            )
            for d in range(1, ZS)
        ]
        for copy in copies:
            copy.start()
        return copies

    def block_at(s):
        r = s % 3
        delta = jnp.where(s < 9, (r * r + r + 1) % 5, 0)
        m = s // 3 - 3 * (s // 9) + (s - 9) * (s // 9)
        there = (y + delta) % 4
        return there, m, 3 * there + m

    def inside(s):
        _, _, k = block_at(s)
        start = pl.multiple_of(k * BLOCK, BLOCK)
        rows = pl.ds(start, BLOCK)
        scores = lax.dot_general(
            cs[rows, :], bs[rows, :], (((1,), (1,)), ((), ())), preferred_element_type=F32
        )
        scores = jnp.where(iota((BLOCK, BLOCK), 0) >= iota((BLOCK, BLOCK), 1), scores, 0.0)
        heads = pl.ds(pl.multiple_of(k * HEADS, HEADS), HEADS)
        across = cum_v[heads, :]
        sizes = step_v[heads, :]
        down = across.T
        left = iota((BLOCK, 128), 1) < HEAD_DIM
        for pair in range(HEADS // 2):
            lanes = pl.ds(pair * 128, 128)
            weights = []
            for h in (2 * pair, 2 * pair + 1):
                gap = jnp.minimum(down[:, h : h + 1] - across[h : h + 1, :], 0.0)
                weights.append((scores * jnp.exp(gap) * sizes[h : h + 1, :]).astype(BF16))
            value = xs[rows, lanes]
            none = jnp.zeros_like(value)
            both = jnp.concatenate([jnp.where(left, value, none), jnp.where(left, none, value)], 0)
            y0[rows, lanes] = dot(jnp.concatenate(weights, 1), both) + skip_v[0:1, lanes] * value.astype(F32)

    def finish(k):
        start = pl.multiple_of(k * BLOCK, BLOCK)
        rows = pl.ds(start, BLOCK)
        squares = jnp.zeros((BLOCK, 128), F32)
        for q in range(PARTS):
            part = pl.ds(q * WIDE, WIDE)
            state_in = entering[k, :, part].astype(F32) + rows_v[pl.ds(16 + k, 1), part] * incoming[q].astype(F32)
            from_state = dot(cs[rows, :], state_in.astype(BF16))
            decay = lax.dot_general(
                decays[k], spread[:, part], (((0,), (0,)), ((), ())), preferred_element_type=F32
            )
            value = (y0[rows, part] + decay * from_state) * silu(gate[rows, part].astype(F32))
            gated_v[:, part] = value
            square = value * value
            squares += square[:, :128] + square[:, 128:]
        scale = lax.rsqrt(jnp.sum(squares, 1, keepdims=True) / COLS + EPSILON)
        for q in range(PARTS):
            part = pl.ds(q * WIDE, WIDE)
            staged[rows, part] = (gated_v[:, part] * scale * gain[0:1, part]).astype(BF16)

    mine = pl.ds(pl.multiple_of(me * COLS, COLS), COLS)

    def send_of(s, i):
        there, m, k = block_at(s)
        j = 2 * m + i
        return pltpu.make_async_remote_copy(
            src_ref=staged.at[pl.ds(pl.multiple_of(k * BLOCK + i * SUB, SUB), SUB)],
            dst_ref=out.at[pl.ds(pl.multiple_of((j % 3) * SUB, SUB), SUB), mine],
            send_sem=y_s.at[2 * s + i], recv_sem=y_r.at[me, j % 3],
            device_id=(c, 2 * there + j // 3), device_id_type=MESH,
        )

    def own_of(s, i):
        _, m, k = block_at(s)
        j = 2 * m + i
        return pltpu.make_async_copy(
            staged.at[pl.ds(pl.multiple_of(k * BLOCK + i * SUB, SUB), SUB)],
            out.at[pl.ds(pl.multiple_of((j % 3) * SUB, SUB), SUB), mine],
            own_sem.at[j % 3],
        )

    def is_own(s, i):
        _, m, _ = block_at(s)
        return (2 * m + i) // 3 == core

    first, second, third = {}, {}, {}
    rings = None
    for q in range(PARTS):
        first[q] = local_states(q)
        if q == 0:
            rings = shard_decays()
        if q >= 1:
            second[q - 1] = along_z(q - 1, first[q - 1])
        if q == 1:
            ring_decays(rings)
        if q >= 2:
            third[q - 2] = along_x(q - 2, second[q - 2])

    def insides(low, high):
        @pl.loop(low, high)
        def _(s):
            inside(s)

    third[PARTS - 2] = along_x(PARTS - 2, second[PARTS - 2])
    insides(0, 4)
    second[PARTS - 1] = along_z(PARTS - 1, first[PARTS - 1])
    insides(4, 8)
    third[PARTS - 1] = along_x(PARTS - 1, second[PARTS - 1])
    insides(8, 12)
    loads[2 + PARTS].wait()
    for q in range(PARTS):
        for copy in third[q]:
            copy.wait()

    @pl.loop(0, 9)
    def _(s):
        _, _, k = block_at(s)
        finish(k)
        for i in range(2):
            send_of(s, i).start()

    @pl.loop(9, 12)
    def _(s):
        _, _, k = block_at(s)
        finish(k)
        for i in range(2):

            @pl.when(is_own(s, i))
            def _():
                own_of(s, i).start()

            @pl.when(jnp.logical_not(is_own(s, i)))
            def _():
                send_of(s, i).start()

    @pl.loop(0, 9)
    def _(s):
        for i in range(2):
            send_of(s, i).wait_send()

    @pl.loop(9, 12)
    def _(s):
        for i in range(2):

            @pl.when(is_own(s, i))
            def _():
                own_of(s, i).wait()

            @pl.when(jnp.logical_not(is_own(s, i)))
            def _():
                send_of(s, i).wait_send()

    @pl.loop(1, 8)
    def _(d):
        source = (me + d) % 8
        lanes = pl.ds(pl.multiple_of(source * COLS, COLS), COLS)
        for j in range(3):
            pltpu.make_async_remote_copy(
                src_ref=staged.at[pl.ds(0, SUB)], dst_ref=out.at[pl.ds(j * SUB, SUB), lanes],
                send_sem=y_s.at[0], recv_sem=y_r.at[source, j],
                device_id=(c, source), device_id_type=MESH,
            ).wait_recv()


def per_device(
    channels_in,
    state_maps,
    gate_in,
    step_raw,
    convolution_channel_taps,
    conv_maps,
    head_rates,
    skip_gain,
    norm_gain,
):
    anywhere = pl.BlockSpec(memory_space=pl.ANY)
    near = pl.BlockSpec(memory_space=pltpu.VMEM)
    dma = pltpu.SemaphoreType.DMA
    return pl.pallas_call(
        kernel,
        out_shape=jax.ShapeDtypeStruct((ROWS // 8, COLS * 8), BF16),
        in_specs=[anywhere] * 4 + [near] * 5,
        out_specs=anywhere,
        scratch_shapes=[
            pltpu.VMEM((LEAD + ROWS, COLS), BF16),
            pltpu.VMEM((LEAD + ROWS, 2 * STATE), BF16),
            pltpu.VMEM((ROWS, COLS), BF16),
            pltpu.VMEM((ROWS, HEADS), F32),
            pltpu.VMEM((LEAD + BLOCK, 128), F32),
            pltpu.VMEM((ROWS, COLS), BF16),
            pltpu.VMEM((ROWS, STATE), BF16),
            pltpu.VMEM((BLOCKS, STATE, BLOCK), BF16),
            pltpu.VMEM((ROWS, STATE), BF16),
            pltpu.VMEM((BLOCKS * HEADS, BLOCK), F32),
            pltpu.VMEM((BLOCKS * HEADS, BLOCK), F32),
            pltpu.VMEM((BLOCKS, 2 * HEADS, BLOCK), BF16),
            pltpu.VMEM((BLOCKS, 2 * HEADS, BLOCK), BF16),
            pltpu.VMEM((2 * HEADS, COLS), BF16),
            pltpu.VMEM((32, COLS), F32),
            pltpu.VMEM((8, COLS), F32),
            pltpu.VMEM((STATE, WIDE), F32),
            pltpu.VMEM((BLOCKS, STATE, COLS), BF16),
            pltpu.VMEM((ROWS, COLS), F32),
            pltpu.VMEM((ROWS, COLS), BF16),
            pltpu.VMEM((BLOCK, COLS), F32),
            pltpu.VMEM((PARTS, STATE, WIDE), BF16),
            pltpu.VMEM((PARTS, ZS, SLICE, WIDE), BF16),
            pltpu.VMEM((PARTS, ZS, SLICE, WIDE), F32),
            pltpu.VMEM((PARTS, SLICE, WIDE), BF16),
            pltpu.VMEM((PARTS, XS, SLICE, WIDE), BF16),
            pltpu.VMEM((PARTS, ZS, SLICE, WIDE), BF16),
            pltpu.VMEM((PARTS, STATE, WIDE), BF16),
            pltpu.VMEM((8, 128), F32),
            pltpu.VMEM((ZS, 8, 128), F32),
            pltpu.VMEM((8, 128), F32),
            pltpu.VMEM((XS, 8, 128), F32),
            pltpu.VMEM((2 * ZS, COLS), F32),
            pltpu.VMEM((8, COLS), F32),
            dma((3 + PARTS,)),
            dma((2,)), dma((2,)),
            dma((ZS,)), dma((ZS,)),
            dma((XS,)), dma((XS,)),
            dma((PARTS, ZS)), dma((PARTS, ZS)),
            dma((PARTS, XS)), dma((PARTS, XS)),
            dma((PARTS, ZS)), dma((PARTS, ZS)),
            dma((24,)), dma((8, 3)), dma((3,)),
        ],
        compiler_params=pltpu.CompilerParams(
            collective_id=0, has_side_effects=True, vmem_limit_bytes=56 * 2**20
        ),
    )(
        channels_in,
        state_maps.reshape(ROWS, 2 * STATE),
        gate_in,
        step_raw,
        convolution_channel_taps,
        conv_maps.reshape(TAPS, 2 * STATE),
        head_rates,
        skip_gain.reshape(1, HEADS),
        norm_gain.reshape(1, COLS),
    )


def solution(mesh):
    return jax.shard_map(
        per_device,
        mesh=mesh,
        in_specs=(
            P("ctx", "head"),
            P("ctx", None, "head"),
            P("ctx", "head"),
            P("ctx", "head"),
            P(None, "head"),
            P(None, None, "head"),
            P(None, "head"),
            P("head"),
            P("head"),
        ),
        out_specs=P(("ctx", "head"), None),
        check_vma=False,
    )
```

time: 662 us -> 94.1 us (0.14)
  the two profiles are of different devices: /device:TPU:6 before, /device:TPU:1 now
where the time goes in v1:
time: 94.1 us; the launch traced here: 93.9 us
  Pallas kernels  84.6 us (90%)
  local copies, waits for them, and re-layouts  9.28 us (10%)
    pallas_call x1, Pallas kernels, per_device(): pl.pallas_call(kernel, out_shape=jax.ShapeDtypeStruct((ROWS // 8, COLS *...  84.6 us
    unnamed x4, local copies, waits for them, and re-layouts  9.28 us

profile of v1, /device:TPU:1, one launch (start us, length us, event | category | flops | bytes accessed | tf_op | source)
XLA Modules:
  0.0 93.9 jit_solution(10985896488269954438)
XLA Ops:
  0.0 1.3 %copy.16 = f32[1,4,2,128]{3,1,2,0:T(4,128)} copy(f32[1,4,2,128]{3,2,1,0:T(2,128)} %bitcast.14) | data formatting | bytes 8192
  1.3 2.1 %copy.15 = bf16[192,8,2,128]{3,1,2,0:T(8,128)(2,1)} copy(bf16[192,8,2,128]{3,2,1,0:T(2,128)(2,1)} %bitcast.11) | data formatting | bytes 1572864
  3.4 2.0 %copy.10.step_hbm = f32[1536,16]{1,0:T(8,128)} copy(f32[1536,16]{0,1:T(8,128)} %param.12) | data formatting | bytes 196608 | tf_op args[3]
  5.4 84.6 %shard_map.91 = bf16[192,8192]{1,0:T(8,128)(2,1)} custom-call(bf16[1536,1024]{1,0:T(8,128)(2,1)} %ch_hbm.1, bf16[1536,256]{1,0:T(8,128)(2,1)} %bitcast.10, bf16[1536,1024]{1,0:T(8,128)(2,1)} %gate_hbm.1, f32[1536,16]{1,0:T(8,128)} %copy.10.step_hbm, f32[4,1024]{1,0:T(4,128)} %taps.1, f32[4,256]{1,0:T(4,128)} %bitcast.12, f32[2,16]{1,0:T(2,128)} %rates.1, ...), custom_call_target="tpu_custom_call" | custom-call | tf_op jit(solution)/shard_map/pallas_call | solution.py:449
  90.0 3.9 %copy.18 = bf16[192,8192]{1,0:T(8,128)(2,1)} copy(bf16[192,8192]{1,0:T(8,128)(2,1)} %shard_map.91) | data formatting | bytes 6291456

commit v2 on v1

v2 whole, which is shorter than its diff:
```python
import jax
import jax.numpy as jnp
from jax import lax
from jax.experimental import pallas as pl
from jax.experimental.pallas import tpu as pltpu
from jax.sharding import PartitionSpec as P

HEAD_DIM = 64
STATE = 128
TAPS = 4
EPSILON = 1e-05
HI = lax.Precision.HIGHEST
MESH = pl.DeviceIdType.MESH
F32 = jnp.float32
BF16 = jnp.bfloat16

ROWS = 1536
COLS = 1024
HEADS = 16
BLOCK = 128
BLOCKS = ROWS // BLOCK
PARTS = 8
WIDE = COLS // PARTS
ZS = 8
XS = 4
SLICE = STATE // ZS
LEAD = 16
TARGET = ROWS // 8
PER = WIDE // HEAD_DIM
PASS = 3


def iota(shape, dim):
    return lax.broadcasted_iota(jnp.int32, shape, dim)


def dot(a, b, precision=None):
    return jnp.dot(a, b, precision=precision, preferred_element_type=F32)


def silu(v):
    half = 0.5 * v
    return half + half * jnp.tanh(half)


def split_in_two(v):
    high = v.astype(BF16).astype(F32)
    return high, v - high


def kernel(
    ch_hbm, bc_hbm, gate_hbm, step_hbm, taps, map_taps, rates, skip, gain, out,
    ch, bc, gate, step, wide, xs, bs, bt, cs, cum_v, step_v, tails, columns, spread,
    rows_v, skip_v, first_v, entering, scores_v, y0, squares, staged, landed,
    zs, z1, prefix, xt, x1, back, base, dl, dl_in, tl, tl_in, za, xa, scale_v, scale_in, scale_w,
    in_sem, halo_s, halo_r, dl_s, dl_r, tl_s, tl_r, z1_s, z1_r, x1_s, x1_r, z2_s, z2_r,
    y_s, y_r, own_sem, n_s, n_r,
):
    c = lax.axis_index("ctx")
    me = lax.axis_index("head")
    x, z = c // ZS, c % ZS
    y, core = me // 2, me % 2

    rest = pl.ds(WIDE, COLS - WIDE)
    loads = [
        pltpu.make_async_copy(step_hbm, step, in_sem.at[0]),
        pltpu.make_async_copy(bc_hbm, bc.at[pl.ds(LEAD, ROWS)], in_sem.at[1]),
        pltpu.make_async_copy(ch_hbm.at[:, pl.ds(0, WIDE)], ch.at[pl.ds(LEAD, ROWS), pl.ds(0, WIDE)], in_sem.at[2]),
        pltpu.make_async_copy(ch_hbm.at[:, rest], ch.at[pl.ds(LEAD, ROWS), rest], in_sem.at[3]),
        pltpu.make_async_copy(gate_hbm, gate, in_sem.at[4]),
    ]
    for load in loads[:3]:
        load.start()

    def z_peer(d):
        return (x * ZS + (z + d) % ZS, me)

    def x_peer(d):
        return (((x + d) % XS) * ZS + z, me)

    after, before = ((c + 1) % (XS * ZS), me), ((c + XS * ZS - 1) % (XS * ZS), me)
    peers = [z_peer(d) for d in range(1, ZS)] + [x_peer(d) for d in range(1, XS)]
    peers += [(c, (me + d) % 8) for d in range(1, 8)] + [after, before]
    barrier = pltpu.get_barrier_semaphore()
    for peer in peers:
        pl.semaphore_signal(barrier, inc=1, device_id=peer, device_id_type=MESH)

    spread[...] = (iota((2 * HEADS, COLS), 0) % HEADS == iota((2 * HEADS, COLS), 1) // HEAD_DIM).astype(BF16)
    head_of = (iota((HEADS, COLS), 0) == iota((HEADS, COLS), 1) // HEAD_DIM).astype(F32)
    bias = jnp.broadcast_to(rates[0:1, :], (BLOCK, HEADS)).T
    rate = jnp.broadcast_to(jnp.exp(rates[1:2, :]), (BLOCK, HEADS)).T
    rate = jnp.concatenate([rate] * BLOCKS, 0)
    loads[0].wait()
    raw = jnp.concatenate([step[:, pl.ds(k * BLOCK, BLOCK)] + bias for k in range(BLOCKS)], 0)
    sizes = jnp.maximum(raw, 0.0) + jnp.log1p(jnp.exp(-jnp.abs(raw)))
    logs = -rate * sizes
    row, col = iota((BLOCK, BLOCK), 0), iota((BLOCK, BLOCK), 1)
    cum = dot(logs, (row <= col).astype(F32), HI)
    later = dot(logs, (row > col).astype(F32), HI)
    cum_v[...] = cum
    step_v[...] = sizes
    high, low = split_in_two(jnp.exp(later) * sizes)
    for k in range(BLOCKS):
        of = slice(k * HEADS, (k + 1) * HEADS)
        tails[k] = jnp.concatenate([high[of], low[of]], 0).T.astype(BF16)
    count = BLOCKS * HEADS
    own_head = (iota((count, HEADS), 0) % HEADS == iota((count, HEADS), 1)).astype(F32)
    own_block = (iota((16, count), 0) == iota((16, count), 1) // HEADS).astype(F32)
    totals = dot(own_block, cum[:, BLOCK - 1 : BLOCK] * own_head, HI)
    row, col = iota((16, 16), 0), iota((16, 16), 1)
    earlier = dot(((row > col) & (col > 0)).astype(F32), totals, HI)
    growth = jnp.exp(dot(jnp.concatenate([totals, earlier], 0), head_of, HI))
    for q in range(PARTS):
        rows_v[q] = growth[:, q * WIDE : (q + 1) * WIDE]
    skip_v[...] = dot(jnp.broadcast_to(skip[...], (8, HEADS)), head_of, HI)
    whole = jnp.broadcast_to(earlier[BLOCKS : BLOCKS + 1] + totals[0:1], (8, HEADS))
    dl[...] = dot(whole, (iota((HEADS, 128), 0) == iota((HEADS, 128), 1)).astype(F32), HI)

    pl.semaphore_wait(barrier, len(peers))
    halo = [
        pltpu.make_async_remote_copy(
            src_ref=source.at[pl.ds(ROWS - LEAD, LEAD)], dst_ref=held.at[pl.ds(0, LEAD)],
            send_sem=halo_s.at[i], recv_sem=halo_r.at[i], device_id=after, device_id_type=MESH,
        )
        for i, (source, held) in enumerate(((bc_hbm, bc), (ch_hbm, ch)))
    ]
    for copy in halo:
        copy.start()
    dl_in[z] = dl[...]
    dl_copies = [
        pltpu.make_async_remote_copy(
            src_ref=dl, dst_ref=dl_in.at[z], send_sem=dl_s.at[d], recv_sem=dl_r.at[d],
            device_id=z_peer(d), device_id_type=MESH,
        )
        for d in range(1, ZS)
    ]
    for copy in dl_copies:
        copy.start()
    for load in loads[3:]:
        load.start()

    def conv(held, start, weight):
        total = weight(0) * held[pl.ds(start + LEAD - 3, BLOCK), :]
        for tap in range(1, TAPS):
            total += weight(tap) * held[pl.ds(start + LEAD - 3 + tap, BLOCK), :]
        return silu(total)

    def maps(k):
        start = k * BLOCK
        rows = pl.ds(start, BLOCK)
        b = conv(wide.at[0], start, lambda tap: map_taps[tap, 0:1, :])
        bs[rows, :] = b.astype(BF16)
        bt[k] = b.T.astype(BF16)
        c_map = conv(wide.at[1], start, lambda tap: map_taps[tap, 1:2, :]).astype(BF16)
        cs[rows, :STATE] = c_map
        cs[rows, STATE:] = c_map

    body, lead = pl.ds(LEAD, ROWS), pl.ds(0, LEAD)
    loads[1].wait()
    for i in range(2):
        wide[i, body, :] = bc[body, pl.ds(i * STATE, STATE)].astype(F32)
    for k in range(1, BLOCKS):
        maps(k)

    def lanes_of(q):
        return pl.ds(pl.multiple_of(q * WIDE, WIDE), WIDE)

    def summary(q, k):
        part = lanes_of(q)
        weights = dot(tails[k], spread[:, part])
        value = conv(wide.at[2], k * BLOCK, lambda tap: taps[tap : tap + 1, part]).astype(BF16)
        xs[q, pl.ds(k * BLOCK, BLOCK), :] = value
        return dot(bt[k], (value.astype(F32) * weights).astype(BF16))

    def blocks_but_first(q):
        part = lanes_of(q)
        wide[2, body, :] = ch[body, part].astype(F32)
        state = jnp.zeros((STATE, WIDE), F32)
        entering[q, 0] = state
        for k in range(1, BLOCKS):
            entering[q, k] = state
            state = rows_v[q, k : k + 1, :] * state + summary(q, k)
        zs[q] = state

    mine = pl.ds(pl.multiple_of(z * SLICE, SLICE), SLICE)

    def z1_copies(q):
        copies = []
        for d in (4, 3, 5, 2, 6, 1, 7):
            there = pl.ds(pl.multiple_of(((z + d) % ZS) * SLICE, SLICE), SLICE)
            copies.append(
                pltpu.make_async_remote_copy(
                    src_ref=xt.at[q, there], dst_ref=z1.at[q, z], send_sem=z1_s.at[q, d],
                    recv_sem=z1_r.at[q, d], device_id=z_peer(d), device_id_type=MESH,
                )
            )
        return copies

    def x1_copies(q):
        return [
            pltpu.make_async_remote_copy(
                src_ref=x1.at[q, x], dst_ref=x1.at[q, x], send_sem=x1_s.at[q, d],
                recv_sem=x1_r.at[q, d], device_id=x_peer(d), device_id_type=MESH,
            )
            for d in (2, 1, 3)
        ]

    def z2_copies(q):
        return [
            pltpu.make_async_remote_copy(
                src_ref=back.at[q, (z + d) % ZS], dst_ref=base.at[q, 0, mine], send_sem=z2_s.at[q, d],
                recv_sem=z2_r.at[q, d], device_id=z_peer(d), device_id_type=MESH,
            )
            for d in (4, 3, 5, 2, 6, 1, 7)
        ]

    def first_block(q):
        part = lanes_of(q)
        wide[2, lead, :] = ch[lead, part].astype(F32)
        first = summary(q, 0)
        first_v[q] = first
        state = (zs[q] + rows_v[q, 16 + BLOCKS : 17 + BLOCKS, :] * first).astype(BF16)
        xt[q] = state
        z1[q, z] = xt[q, mine, :]
        for copy in z1_copies(q):
            copy.start()

    def shard_decays():
        for copy in dl_copies:
            copy.wait()
        each = jnp.concatenate([dl_in[i, 0:1, :] for i in range(ZS)], 0)
        ahead = dot((iota((ZS, ZS), 0) > iota((ZS, ZS), 1)).astype(F32), each, HI)
        both = jnp.concatenate([each, ahead], 0)
        za[...] = jnp.exp(dot(both[:, :HEADS], head_of, HI))
        tl[...] = jnp.broadcast_to(jnp.sum(each, 0, keepdims=True), (8, 128))
        tl_in[x] = tl[...]
        copies = [
            pltpu.make_async_remote_copy(
                src_ref=tl, dst_ref=tl_in.at[x], send_sem=tl_s.at[d], recv_sem=tl_r.at[d],
                device_id=x_peer(d), device_id_type=MESH,
            )
            for d in range(1, XS)
        ]
        for copy in copies:
            copy.start()
        return copies

    def ring_decays(copies):
        for copy in copies:
            copy.wait()
        each = jnp.concatenate([tl_in[i, 0:1, :] for i in range(XS)] * 2, 0)
        xa[...] = jnp.exp(dot(each[:, :HEADS], head_of, HI))

    def along_z(q):
        part = lanes_of(q)
        for copy in z1_copies(q):
            copy.wait()
        total = jnp.zeros((SLICE, WIDE), F32)
        for i in range(ZS):
            prefix[q, i] = total
            total = za[i : i + 1, part] * total + z1[q, i].astype(F32)
        x1[q, x] = total
        for copy in x1_copies(q):
            copy.start()

    def along_x(q):
        part = lanes_of(q)
        for copy in x1_copies(q):
            copy.wait()
        total = jnp.zeros((SLICE, WIDE), F32)
        for i in range(XS - 1):
            total = jnp.where(i < x, xa[i : i + 1, part] * total + x1[q, i], total)
        for i in range(ZS):
            back[q, i] = prefix[q, i] + za[ZS + i : ZS + i + 1, part] * total
        base[q, 0, mine, :] = back[q, z]
        for copy in z2_copies(q):
            copy.start()

    def blocks_alone():
        @pl.loop(0, BLOCKS)
        def _(k):
            rows = pl.ds(pl.multiple_of(k * BLOCK, BLOCK), BLOCK)
            scores = lax.dot_general(
                cs[rows, :STATE], bs[rows, :], (((1,), (1,)), ((), ())), preferred_element_type=F32
            )
            scores_v[k] = jnp.where(iota((BLOCK, BLOCK), 0) >= iota((BLOCK, BLOCK), 1), scores, 0.0)
            sums = cum_v[pl.ds(pl.multiple_of(k * HEADS, HEADS), HEADS), :]
            high, low = split_in_two(sums)
            middle, low = split_in_two(low)
            parts = [high, middle, low, *split_in_two(jnp.exp(sums))]
            columns[k] = jnp.concatenate(parts, 0).T.astype(BF16)

    def inside(q):
        part = lanes_of(q)
        left = iota((BLOCK, WIDE), 1) < HEAD_DIM
        pick = PER * q + iota((3 * HEADS, PER * BLOCK), 1) // BLOCK == iota((3 * HEADS, PER * BLOCK), 0) % HEADS
        pick = pick.astype(BF16)

        @pl.loop(0, BLOCKS // 3)
        def _(j):
            for i in range(3):
                k = 3 * j + i
                rows = pl.ds(pl.multiple_of(k * BLOCK, BLOCK), BLOCK)
                down = dot(columns[k, :, : 3 * HEADS], pick)
                weights = []
                for h in range(PER):
                    at = pl.ds(k * HEADS + PER * q + h, 1)
                    gap = jnp.minimum(down[:, h * BLOCK : (h + 1) * BLOCK] - cum_v[at, :], 0.0)
                    weights.append((scores_v[k] * jnp.exp(gap) * step_v[at, :]).astype(BF16))
                value = xs[q, rows, :]
                none = jnp.zeros_like(value)
                both = jnp.concatenate([jnp.where(left, value, none), jnp.where(left, none, value)], 0)
                y0[rows, :] = dot(jnp.concatenate(weights, 1), both) + skip_v[0:1, part] * value.astype(F32)

    def send_of(q, t, to):
        delta = (t * t + t + 1) % 5 * (1 - t // 3)
        there = (y + delta) % 4
        return pltpu.make_async_remote_copy(
            src_ref=staged.at[q, pl.ds(pl.multiple_of((2 * there + to) * TARGET, TARGET), TARGET)],
            dst_ref=landed.at[me, q], send_sem=y_s.at[q, t, to], recv_sem=y_r.at[q, me],
            device_id=(c, 2 * there + to), device_id_type=MESH,
        )

    def own_of(q):
        return pltpu.make_async_copy(
            staged.at[q, pl.ds(pl.multiple_of(me * TARGET, TARGET), TARGET)],
            landed.at[me, q], own_sem.at[q],
        )

    def scale_of(t, to):
        delta = (t * t + t + 1) % 5 * (1 - t // 3)
        there = (y + delta) % 4
        return pltpu.make_async_remote_copy(
            src_ref=scale_v.at[there], dst_ref=scale_in.at[me], send_sem=n_s.at[t, to],
            recv_sem=n_r.at[me], device_id=(c, 2 * there + to), device_id_type=MESH,
        )

    def all_but_own(t, to, remote, own):
        @pl.when((t < 3) | (to != core))
        def _():
            remote()

        @pl.when((t == 3) & (to == core))
        def _():
            own()

    def finish(q):
        part = lanes_of(q)
        for copy in z2_copies(q):
            copy.wait()
        base[q, 1] = rows_v[q, 0:1, :] * base[q, 0] + first_v[q]

        @pl.loop(0, 4)
        def _(t):
            delta = (t * t + t + 1) % 5 * (1 - t // 3)
            there = (y + delta) % 4
            for m in range(PASS):
                k = PASS * there + m
                rows = pl.ds(pl.multiple_of(k * BLOCK, BLOCK), BLOCK)
                state_in = entering[q, k] + rows_v[q, pl.ds(16 + k, 1), :] * base[q, jnp.minimum(k, 1)]
                high, low = split_in_two(state_in)
                from_state = dot(cs[rows, :], jnp.concatenate([high, low], 0).astype(BF16))
                decay = dot(columns[k, :, 3 * HEADS :], spread[:, part])
                value = (y0[rows, :] + decay * from_state) * silu(gate[rows, part].astype(F32))
                square = jnp.where(q == 0, 0.0, squares[rows, :]) + value * value
                squares[rows, :] = square
                staged[q, rows, :] = (value * gain[0:1, part]).astype(BF16)
                if m > 0:
                    to = m - 1
                    all_but_own(t, to, send_of(q, t, to).start, own_of(q).start)

    def scales():
        @pl.loop(0, 4)
        def _(t):
            delta = (t * t + t + 1) % 5 * (1 - t // 3)
            there = (y + delta) % 4
            for m in range(PASS):
                rows = pl.ds(pl.multiple_of((PASS * there + m) * BLOCK, BLOCK), BLOCK)
                scale = lax.rsqrt(jnp.sum(squares[rows, :], 1, keepdims=True) / COLS + EPSILON)
                scale_v[there, m] = jnp.broadcast_to(scale, (BLOCK, 128)).T[0:8, :]
            for to in range(2):

                def own():
                    scale_in[me] = scale_v[there]

                all_but_own(t, to, scale_of(t, to).start, own)

    loads[2].wait()
    blocks_but_first(0)
    for copy in halo:
        copy.wait()

    @pl.when(c == 0)
    def _():
        bc[lead, :] = jnp.zeros((LEAD, 2 * STATE), BF16)
        ch[lead, :] = jnp.zeros((LEAD, COLS), BF16)

    for i in range(2):
        wide[i, lead, :] = bc[lead, pl.ds(i * STATE, STATE)].astype(F32)
    maps(0)
    first_block(0)
    loads[3].wait()

    def steps(low, high, *more):
        @pl.loop(low, high)
        def _(q):
            blocks_but_first(q)
            first_block(q)
            for what, lag in more:
                what(q - lag)

    steps(1, 3)
    rings = shard_decays()
    steps(3, 5, (along_z, 3))
    ring_decays(rings)
    steps(5, PARTS, (along_z, 3), (along_x, 5))
    blocks_alone()
    loads[4].wait()

    @pl.loop(0, PARTS)
    def _(q):
        inside(q)
        finish(q)

        @pl.when(q < 3)
        def _():
            along_z(q + PARTS - 3)

        @pl.when(q < 5)
        def _():
            along_x(q + PARTS - 5)

    scales()

    def place(source):
        for m in range(PASS):
            scale_w[pl.ds(m * BLOCK, BLOCK), :] = jnp.broadcast_to(scale_in[source, m, 0:1, :], (128, BLOCK)).T
        scale = scale_w[pl.ds(pl.multiple_of(core * TARGET, TARGET), TARGET), :]
        for q in range(PARTS):
            lanes = pl.ds(pl.multiple_of(source * COLS + q * WIDE, WIDE), WIDE)
            out[:, lanes] = (landed[source, q].astype(F32) * scale).astype(BF16)

    for q in range(PARTS):
        own_of(q).wait()
    place(me)

    @pl.loop(1, 8)
    def _(d):
        source = (me + d) % 8
        for q in range(PARTS):
            pltpu.make_async_remote_copy(
                src_ref=staged.at[q, pl.ds(0, TARGET)], dst_ref=landed.at[source, q],
                send_sem=y_s.at[q, 0, 0], recv_sem=y_r.at[q, source],
                device_id=(c, source), device_id_type=MESH,
            ).wait_recv()
        pltpu.make_async_remote_copy(
            src_ref=scale_v.at[0], dst_ref=scale_in.at[source], send_sem=n_s.at[0, 0],
            recv_sem=n_r.at[source], device_id=(c, source), device_id_type=MESH,
        ).wait_recv()
        place(source)

    @pl.loop(0, 4)
    def _(t):
        for to in range(2):

            def remote():
                for q in range(PARTS):
                    send_of(q, t, to).wait_send()
                scale_of(t, to).wait_send()

            all_but_own(t, to, remote, lambda: None)


def per_device(
    channels_in,
    state_maps,
    gate_in,
    step_raw,
    convolution_channel_taps,
    conv_maps,
    head_rates,
    skip_gain,
    norm_gain,
):
    anywhere = pl.BlockSpec(memory_space=pl.ANY)
    near = pl.BlockSpec(memory_space=pltpu.VMEM)
    dma = pltpu.SemaphoreType.DMA
    return pl.pallas_call(
        kernel,
        out_shape=pltpu.VMEM((TARGET, COLS * 8), BF16),
        in_specs=[anywhere] * 4 + [near] * 5,
        out_specs=near,
        scratch_shapes=[
            pltpu.VMEM((LEAD + ROWS, COLS), BF16),
            pltpu.VMEM((LEAD + ROWS, 2 * STATE), BF16),
            pltpu.VMEM((ROWS, COLS), BF16),
            pltpu.VMEM((HEADS, ROWS), F32),
            pltpu.VMEM((3, LEAD + ROWS, 128), F32),
            pltpu.VMEM((PARTS, ROWS, WIDE), BF16),
            pltpu.VMEM((ROWS, STATE), BF16),
            pltpu.VMEM((BLOCKS, STATE, BLOCK), BF16),
            pltpu.VMEM((ROWS, 2 * STATE), BF16),
            pltpu.VMEM((BLOCKS * HEADS, BLOCK), F32),
            pltpu.VMEM((BLOCKS * HEADS, BLOCK), F32),
            pltpu.VMEM((BLOCKS, BLOCK, 2 * HEADS), BF16),
            pltpu.VMEM((BLOCKS, BLOCK, 5 * HEADS), BF16),
            pltpu.VMEM((2 * HEADS, COLS), BF16),
            pltpu.VMEM((PARTS, 32, WIDE), F32),
            pltpu.VMEM((8, COLS), F32),
            pltpu.VMEM((PARTS, STATE, WIDE), F32),
            pltpu.VMEM((PARTS, BLOCKS, STATE, WIDE), F32),
            pltpu.VMEM((BLOCKS, BLOCK, BLOCK), F32),
            pltpu.VMEM((ROWS, WIDE), F32),
            pltpu.VMEM((ROWS, WIDE), F32),
            pltpu.VMEM((PARTS, ROWS, WIDE), BF16),
            pltpu.VMEM((8, PARTS, TARGET, WIDE), BF16),
            pltpu.VMEM((PARTS, STATE, WIDE), F32),
            pltpu.VMEM((PARTS, ZS, SLICE, WIDE), BF16),
            pltpu.VMEM((PARTS, ZS, SLICE, WIDE), F32),
            pltpu.VMEM((PARTS, STATE, WIDE), BF16),
            pltpu.VMEM((PARTS, XS, SLICE, WIDE), F32),
            pltpu.VMEM((PARTS, ZS, SLICE, WIDE), F32),
            pltpu.VMEM((PARTS, 2, STATE, WIDE), F32),
            pltpu.VMEM((8, 128), F32),
            pltpu.VMEM((ZS, 8, 128), F32),
            pltpu.VMEM((8, 128), F32),
            pltpu.VMEM((XS, 8, 128), F32),
            pltpu.VMEM((2 * ZS, COLS), F32),
            pltpu.VMEM((8, COLS), F32),
            pltpu.VMEM((4, PASS, 8, BLOCK), F32),
            pltpu.VMEM((8, PASS, 8, BLOCK), F32),
            pltpu.VMEM((PASS * BLOCK, 128), F32),
            dma((5,)),
            dma((2,)), dma((2,)),
            dma((ZS,)), dma((ZS,)),
            dma((XS,)), dma((XS,)),
            dma((PARTS, ZS)), dma((PARTS, ZS)),
            dma((PARTS, XS)), dma((PARTS, XS)),
            dma((PARTS, ZS)), dma((PARTS, ZS)),
            dma((PARTS, 4, 2)), dma((PARTS, 8)), dma((PARTS,)),
            dma((4, 2)), dma((8,)),
        ],
        compiler_params=pltpu.CompilerParams(
            collective_id=0, has_side_effects=True, vmem_limit_bytes=60 * 2**20
        ),
    )(
        channels_in,
        state_maps.reshape(ROWS, 2 * STATE),
        gate_in,
        step_raw.T,
        convolution_channel_taps,
        conv_maps,
        head_rates,
        skip_gain.reshape(1, HEADS),
        norm_gain.reshape(1, COLS),
    )


def solution(mesh):
    return jax.shard_map(
        per_device,
        mesh=mesh,
        in_specs=(
            P("ctx", "head"),
            P("ctx", None, "head"),
            P("ctx", "head"),
            P("ctx", "head"),
            P(None, "head"),
            P(None, None, "head"),
            P(None, "head"),
            P("head"),
            P("head"),
        ),
        out_specs=P(("ctx", "head"), None),
        check_vma=False,
    )
```

time: 94.1 us -> 75.7 us (0.80)
  Pallas kernels: 84.6 us -> 71.7 us
  local copies, waits for them, and re-layouts: 9.28 us -> 3.78 us
    pallas_call x1, Pallas kernels: 84.6 us -> 71.7 us  [per_device(): pl.pallas_call(kernel, out_shape=pltpu.VMEM((TARGET, COLS * 8), BF16), in...]
    unnamed x4 -> x2, local copies, waits for them, and re-layouts: 9.28 us -> 3.78 us
where the time goes in v2:
time: 75.7 us; the launch traced here: 75.5 us
  Pallas kernels  71.7 us (95%)
  local copies, waits for them, and re-layouts  3.78 us (5%)
    pallas_call x1, Pallas kernels, per_device(): pl.pallas_call(kernel, out_shape=pltpu.VMEM((TARGET, COLS * 8), BF16), in...  71.7 us
    unnamed x2, local copies, waits for them, and re-layouts  3.78 us

profile of v2, /device:TPU:1, one launch (start us, length us, event | category | flops | bytes accessed | tf_op | source)
XLA Modules:
  0.0 75.5 jit_solution(9247722556061263903)
XLA Ops:
  0.0 2.1 %copy.12 = bf16[192,8,2,128]{3,1,2,0:T(8,128)(2,1)} copy(bf16[192,8,2,128]{3,2,1,0:T(2,128)(2,1)} %bitcast.8) | data formatting | bytes 1572864
  2.1 71.7 %shard_map.91 = bf16[192,8192]{1,0:T(8,128)(2,1)S(1)} custom-call(bf16[1536,1024]{1,0:T(8,128)(2,1)} %ch_hbm.1, bf16[1536,256]{1,0:T(8,128)(2,1)} %bitcast.7, bf16[1536,1024]{1,0:T(8,128)(2,1)} %gate_hbm.1, f32[16,1536]{1,0:T(8,128)} %bitcast.9, f32[4,1024]{1,0:T(4,128)} %taps.1, f32[4,2,128]{2,1,0:T(2,128)} %map_taps.1, f32[2,16]{1,0:T(2,128)} %rates.1, ...), custom_call_target="tpu_custom_call" | custom-call | tf_op jit(solution)/shard_map/pallas_call | solution.py:488
  73.8 1.7 %copy.14 = bf16[192,8192]{1,0:T(8,128)(2,1)} copy(bf16[192,8192]{1,0:T(8,128)(2,1)S(1)} %shard_map.91) | data formatting | bytes 6291456

commit v3 on v2

--- a/solution.py
+++ b/solution.py
@@ -28,6 +28,7 @@
 TARGET = ROWS // 8
 PER = WIDE // HEAD_DIM
 PASS = 3
+HELD = 2
 
 
 def iota(shape, dim):
@@ -50,9 +51,9 @@
 
 def kernel(
     ch_hbm, bc_hbm, gate_hbm, step_hbm, taps, map_taps, rates, skip, gain, out,
-    ch, bc, gate, step, wide, xs, bs, bt, cs, cum_v, step_v, tails, columns, spread,
+    ch, bc, gate, step, wide, wide_maps, xs, bs, bt, cs, cum_v, step_v, tails, columns, spread,
     rows_v, skip_v, first_v, entering, scores_v, y0, squares, staged, landed,
-    zs, z1, prefix, xt, x1, back, base, dl, dl_in, tl, tl_in, za, xa, scale_v, scale_in, scale_w,
+    zs, z1, prefix, xt, x1, back, base, dl, dl_in, tl, tl_in, za, xa, scale_v, scale_in, scale_w, scale_all,
     in_sem, halo_s, halo_r, dl_s, dl_r, tl_s, tl_r, z1_s, z1_r, x1_s, x1_r, z2_s, z2_r,
     y_s, y_r, own_sem, n_s, n_r,
 ):
@@ -64,7 +65,7 @@
     rest = pl.ds(WIDE, COLS - WIDE)
     loads = [
         pltpu.make_async_copy(step_hbm, step, in_sem.at[0]),
-        pltpu.make_async_copy(bc_hbm, bc.at[pl.ds(LEAD, ROWS)], in_sem.at[1]),
+        pltpu.make_async_copy(bc_hbm, bc.at[pl.ds(2 * LEAD, 2 * ROWS)], in_sem.at[1]),
         pltpu.make_async_copy(ch_hbm.at[:, pl.ds(0, WIDE)], ch.at[pl.ds(LEAD, ROWS), pl.ds(0, WIDE)], in_sem.at[2]),
         pltpu.make_async_copy(ch_hbm.at[:, rest], ch.at[pl.ds(LEAD, ROWS), rest], in_sem.at[3]),
         pltpu.make_async_copy(gate_hbm, gate, in_sem.at[4]),
@@ -117,14 +118,18 @@
     dl[...] = dot(whole, (iota((HEADS, 128), 0) == iota((HEADS, 128), 1)).astype(F32), HI)
 
     pl.semaphore_wait(barrier, len(peers))
+    ends = [
+        (bc_hbm.at[pl.ds(2 * (ROWS - LEAD), 2 * LEAD)], bc.at[pl.ds(0, 2 * LEAD)]),
+        *((ch_hbm.at[pl.ds(ROWS - LEAD, LEAD), at], ch.at[pl.ds(0, LEAD), at]) for at in (pl.ds(0, WIDE), rest)),
+    ]
     halo = [
         pltpu.make_async_remote_copy(
-            src_ref=source.at[pl.ds(ROWS - LEAD, LEAD)], dst_ref=held.at[pl.ds(0, LEAD)],
-            send_sem=halo_s.at[i], recv_sem=halo_r.at[i], device_id=after, device_id_type=MESH,
+            src_ref=source, dst_ref=held, send_sem=halo_s.at[i], recv_sem=halo_r.at[i],
+            device_id=after, device_id_type=MESH,
         )
-        for i, (source, held) in enumerate(((bc_hbm, bc), (ch_hbm, ch)))
+        for i, (source, held) in enumerate(ends)
     ]
-    for copy in halo:
+    for copy in halo[:2]:
         copy.start()
     dl_in[z] = dl[...]
     dl_copies = [
@@ -136,29 +141,35 @@
     ]
     for copy in dl_copies:
         copy.start()
+    halo[2].start()
     for load in loads[3:]:
         load.start()
 
-    def conv(held, start, weight):
-        total = weight(0) * held[pl.ds(start + LEAD - 3, BLOCK), :]
+    def conv(row, weight):
+        total = weight(0) * row(LEAD - 3)
         for tap in range(1, TAPS):
-            total += weight(tap) * held[pl.ds(start + LEAD - 3 + tap, BLOCK), :]
+            total += weight(tap) * row(LEAD - 3 + tap)
         return silu(total)
 
     def maps(k):
-        start = k * BLOCK
-        rows = pl.ds(start, BLOCK)
-        b = conv(wide.at[0], start, lambda tap: map_taps[tap, 0:1, :])
+        rows = pl.ds(k * BLOCK, BLOCK)
+
+        def each(i):
+            return conv(
+                lambda r: wide_maps[pl.ds(2 * (k * BLOCK + r) + i, BLOCK, stride=2), :],
+                lambda tap: map_taps[tap, i : i + 1, :],
+            )
+
+        b = each(0)
         bs[rows, :] = b.astype(BF16)
         bt[k] = b.T.astype(BF16)
-        c_map = conv(wide.at[1], start, lambda tap: map_taps[tap, 1:2, :]).astype(BF16)
+        c_map = each(1).astype(BF16)
         cs[rows, :STATE] = c_map
         cs[rows, STATE:] = c_map
 
     body, lead = pl.ds(LEAD, ROWS), pl.ds(0, LEAD)
     loads[1].wait()
-    for i in range(2):
-        wide[i, body, :] = bc[body, pl.ds(i * STATE, STATE)].astype(F32)
+    wide_maps[pl.ds(2 * LEAD, 2 * ROWS), :] = bc[pl.ds(2 * LEAD, 2 * ROWS), :].astype(F32)
     for k in range(1, BLOCKS):
         maps(k)
 
@@ -168,13 +179,15 @@
     def summary(q, k):
         part = lanes_of(q)
         weights = dot(tails[k], spread[:, part])
-        value = conv(wide.at[2], k * BLOCK, lambda tap: taps[tap : tap + 1, part]).astype(BF16)
+        value = conv(
+            lambda r: wide[pl.ds(k * BLOCK + r, BLOCK), :], lambda tap: taps[tap : tap + 1, part]
+        ).astype(BF16)
         xs[q, pl.ds(k * BLOCK, BLOCK), :] = value
         return dot(bt[k], (value.astype(F32) * weights).astype(BF16))
 
     def blocks_but_first(q):
         part = lanes_of(q)
-        wide[2, body, :] = ch[body, part].astype(F32)
+        wide[body, :] = ch[body, part].astype(F32)
         state = jnp.zeros((STATE, WIDE), F32)
         entering[q, 0] = state
         for k in range(1, BLOCKS):
@@ -216,7 +229,7 @@
 
     def first_block(q):
         part = lanes_of(q)
-        wide[2, lead, :] = ch[lead, part].astype(F32)
+        wide[lead, :] = ch[lead, part].astype(F32)
         first = summary(q, 0)
         first_v[q] = first
         state = (zs[q] + rows_v[q, 16 + BLOCKS : 17 + BLOCKS, :] * first).astype(BF16)
@@ -344,7 +357,10 @@
         def _():
             own()
 
-    def finish(q):
+    def ship(q, t, to):
+        all_but_own(t, to, send_of(q, t, to).start, own_of(q).start)
+
+    def finish(q, send):
         part = lanes_of(q)
         for copy in z2_copies(q):
             copy.wait()
@@ -365,9 +381,8 @@
                 square = jnp.where(q == 0, 0.0, squares[rows, :]) + value * value
                 squares[rows, :] = square
                 staged[q, rows, :] = (value * gain[0:1, part]).astype(BF16)
-                if m > 0:
-                    to = m - 1
-                    all_but_own(t, to, send_of(q, t, to).start, own_of(q).start)
+                if send and m > 0:
+                    ship(q, t, m - 1)
 
     def scales():
         @pl.loop(0, 4)
@@ -387,19 +402,23 @@
 
     loads[2].wait()
     blocks_but_first(0)
-    for copy in halo:
+    for copy in halo[:2]:
         copy.wait()
 
     @pl.when(c == 0)
     def _():
-        bc[lead, :] = jnp.zeros((LEAD, 2 * STATE), BF16)
-        ch[lead, :] = jnp.zeros((LEAD, COLS), BF16)
-
-    for i in range(2):
-        wide[i, lead, :] = bc[lead, pl.ds(i * STATE, STATE)].astype(F32)
+        bc[pl.ds(0, 2 * LEAD), :] = jnp.zeros((2 * LEAD, STATE), BF16)
+        ch[lead, pl.ds(0, WIDE)] = jnp.zeros((LEAD, WIDE), BF16)
+
+    wide_maps[pl.ds(0, 2 * LEAD), :] = bc[pl.ds(0, 2 * LEAD), :].astype(F32)
     maps(0)
     first_block(0)
     loads[3].wait()
+    halo[2].wait()
+
+    @pl.when(c == 0)
+    def _():
+        ch[lead, rest] = jnp.zeros((LEAD, COLS - WIDE), BF16)
 
     def steps(low, high, *more):
         @pl.loop(low, high)
@@ -417,10 +436,10 @@
     blocks_alone()
     loads[4].wait()
 
-    @pl.loop(0, PARTS)
+    @pl.loop(0, PARTS - HELD)
     def _(q):
         inside(q)
-        finish(q)
+        finish(q, True)
 
         @pl.when(q < 3)
         def _():
@@ -430,34 +449,54 @@
         def _():
             along_x(q + PARTS - 5)
 
+    for q in range(PARTS - HELD, PARTS):
+        inside(q)
+        finish(q, False)
     scales()
 
-    def place(source):
+    @pl.loop(PARTS - HELD, PARTS)
+    def _(q):
+        @pl.loop(0, 4)
+        def _(t):
+            for to in range(2):
+                ship(q, t, to)
+
+    def spread_scale(source):
         for m in range(PASS):
             scale_w[pl.ds(m * BLOCK, BLOCK), :] = jnp.broadcast_to(scale_in[source, m, 0:1, :], (128, BLOCK)).T
-        scale = scale_w[pl.ds(pl.multiple_of(core * TARGET, TARGET), TARGET), :]
-        for q in range(PARTS):
-            lanes = pl.ds(pl.multiple_of(source * COLS + q * WIDE, WIDE), WIDE)
-            out[:, lanes] = (landed[source, q].astype(F32) * scale).astype(BF16)
-
-    for q in range(PARTS):
+        scale_all[source] = scale_w[pl.ds(pl.multiple_of(core * TARGET, TARGET), TARGET), :]
+
+    def place(source, q):
+        lanes = pl.ds(pl.multiple_of(source * COLS + q * WIDE, WIDE), WIDE)
+        out[:, lanes] = (landed[source, q].astype(F32) * scale_all[source]).astype(BF16)
+
+    spread_scale(me)
+
+    @pl.loop(0, PARTS)
+    def _(q):
         own_of(q).wait()
-    place(me)
+        place(me, q)
 
     @pl.loop(1, 8)
     def _(d):
         source = (me + d) % 8
-        for q in range(PARTS):
+        pltpu.make_async_remote_copy(
+            src_ref=scale_v.at[0], dst_ref=scale_in.at[source], send_sem=n_s.at[0, 0],
+            recv_sem=n_r.at[source], device_id=(c, source), device_id_type=MESH,
+        ).wait_recv()
+        spread_scale(source)
+
+    @pl.loop(0, PARTS)
+    def _(q):
+        @pl.loop(1, 8)
+        def _(d):
+            source = (me + d) % 8
             pltpu.make_async_remote_copy(
                 src_ref=staged.at[q, pl.ds(0, TARGET)], dst_ref=landed.at[source, q],
                 send_sem=y_s.at[q, 0, 0], recv_sem=y_r.at[q, source],
                 device_id=(c, source), device_id_type=MESH,
             ).wait_recv()
-        pltpu.make_async_remote_copy(
-            src_ref=scale_v.at[0], dst_ref=scale_in.at[source], send_sem=n_s.at[0, 0],
-            recv_sem=n_r.at[source], device_id=(c, source), device_id_type=MESH,
-        ).wait_recv()
-        place(source)
+            place(source, q)
 
     @pl.loop(0, 4)
     def _(t):
@@ -492,10 +531,11 @@
         out_specs=near,
         scratch_shapes=[
             pltpu.VMEM((LEAD + ROWS, COLS), BF16),
-            pltpu.VMEM((LEAD + ROWS, 2 * STATE), BF16),
+            pltpu.VMEM((2 * (LEAD + ROWS), STATE), BF16),
             pltpu.VMEM((ROWS, COLS), BF16),
             pltpu.VMEM((HEADS, ROWS), F32),
-            pltpu.VMEM((3, LEAD + ROWS, 128), F32),
+            pltpu.VMEM((LEAD + ROWS, WIDE), F32),
+            pltpu.VMEM((2 * (LEAD + ROWS), STATE), F32),
             pltpu.VMEM((PARTS, ROWS, WIDE), BF16),
             pltpu.VMEM((ROWS, STATE), BF16),
             pltpu.VMEM((BLOCKS, STATE, BLOCK), BF16),
@@ -530,8 +570,9 @@
             pltpu.VMEM((4, PASS, 8, BLOCK), F32),
             pltpu.VMEM((8, PASS, 8, BLOCK), F32),
             pltpu.VMEM((PASS * BLOCK, 128), F32),
+            pltpu.VMEM((8, TARGET, 128), F32),
             dma((5,)),
-            dma((2,)), dma((2,)),
+            dma((3,)), dma((3,)),
             dma((ZS,)), dma((ZS,)),
             dma((XS,)), dma((XS,)),
             dma((PARTS, ZS)), dma((PARTS, ZS)),
@@ -545,7 +586,7 @@
         ),
     )(
         channels_in,
-        state_maps.reshape(ROWS, 2 * STATE),
+        state_maps.reshape(2 * ROWS, STATE),
         gate_in,
         step_raw.T,
         convolution_channel_taps,

time: 75.7 us -> 71.8 us (0.948)
  local copies, waits for them, and re-layouts: 3.78 us -> 1.67 us
  Pallas kernels: 71.7 us -> 70 us
    unnamed x2 -> x1, local copies, waits for them, and re-layouts: 3.78 us -> 1.67 us
    pallas_call x1, Pallas kernels: 71.7 us -> 70 us  [per_device(): pl.pallas_call(kernel, out_shape=pltpu.VMEM((TARGET, COLS * 8), BF16), in...]
where the time goes in v3:
time: 71.8 us; the launch traced here: 71.6 us
  Pallas kernels  70 us (97%)
  local copies, waits for them, and re-layouts  1.67 us (2%)
    pallas_call x1, Pallas kernels, per_device(): pl.pallas_call(kernel, out_shape=pltpu.VMEM((TARGET, COLS * 8), BF16), in...  70 us
    unnamed x1, local copies, waits for them, and re-layouts  1.67 us

profile of v3, /device:TPU:1, one launch (start us, length us, event | category | flops | bytes accessed | tf_op | source)
XLA Modules:
  0.0 71.6 jit_solution(2716789696639274931)
XLA Ops:
  0.0 70.0 %shard_map.91 = bf16[192,8192]{1,0:T(8,128)(2,1)S(1)} custom-call(bf16[1536,1024]{1,0:T(8,128)(2,1)} %ch_hbm.1, bf16[3072,128]{1,0:T(8,128)(2,1)} %bitcast.4, bf16[1536,1024]{1,0:T(8,128)(2,1)} %gate_hbm.1, f32[16,1536]{1,0:T(8,128)} %bitcast.5, f32[4,1024]{1,0:T(4,128)} %taps.1, f32[4,2,128]{2,1,0:T(2,128)} %map_taps.1, f32[2,16]{1,0:T(2,128)} %rates.1, ...), custom_call_target="tpu_custom_call" | custom-call | tf_op jit(solution)/shard_map/pallas_call | solution.py:527
  70.0 1.7 %copy.11 = bf16[192,8192]{1,0:T(8,128)(2,1)} copy(bf16[192,8192]{1,0:T(8,128)(2,1)S(1)} %shard_map.91) | data formatting | bytes 6291456

commit v4 on v3

--- a/solution.py
+++ b/solution.py
@@ -28,7 +28,8 @@
 TARGET = ROWS // 8
 PER = WIDE // HEAD_DIM
 PASS = 3
-HELD = 2
+HELD = 1
+UNROLL = 4
 
 
 def iota(shape, dim):
@@ -98,7 +99,7 @@
     row, col = iota((BLOCK, BLOCK), 0), iota((BLOCK, BLOCK), 1)
     cum = dot(logs, (row <= col).astype(F32), HI)
     later = dot(logs, (row > col).astype(F32), HI)
-    cum_v[...] = cum
+    cum_v[...] = cum * 1.4426950408889634
     step_v[...] = sizes
     high, low = split_in_two(jnp.exp(later) * sizes)
     for k in range(BLOCKS):
@@ -228,9 +229,10 @@
         ]
 
     def first_block(q):
-        part = lanes_of(q)
-        wide[lead, :] = ch[lead, part].astype(F32)
-        first = summary(q, 0)
+        wide[lead, :] = ch[lead, lanes_of(q)].astype(F32)
+        leave(q, summary(q, 0))
+
+    def leave(q, first):
         first_v[q] = first
         state = (zs[q] + rows_v[q, 16 + BLOCKS : 17 + BLOCKS, :] * first).astype(BF16)
         xt[q] = state
@@ -290,18 +292,20 @@
             copy.start()
 
     def blocks_alone():
-        @pl.loop(0, BLOCKS)
-        def _(k):
-            rows = pl.ds(pl.multiple_of(k * BLOCK, BLOCK), BLOCK)
-            scores = lax.dot_general(
-                cs[rows, :STATE], bs[rows, :], (((1,), (1,)), ((), ())), preferred_element_type=F32
-            )
-            scores_v[k] = jnp.where(iota((BLOCK, BLOCK), 0) >= iota((BLOCK, BLOCK), 1), scores, 0.0)
-            sums = cum_v[pl.ds(pl.multiple_of(k * HEADS, HEADS), HEADS), :]
-            high, low = split_in_two(sums)
-            middle, low = split_in_two(low)
-            parts = [high, middle, low, *split_in_two(jnp.exp(sums))]
-            columns[k] = jnp.concatenate(parts, 0).T.astype(BF16)
+        @pl.loop(0, BLOCKS // UNROLL)
+        def _(j):
+            for i in range(UNROLL):
+                k = UNROLL * j + i
+                rows = pl.ds(pl.multiple_of(k * BLOCK, BLOCK), BLOCK)
+                scores = lax.dot_general(
+                    cs[rows, :STATE], bs[rows, :], (((1,), (1,)), ((), ())), preferred_element_type=F32
+                )
+                scores_v[k] = jnp.where(iota((BLOCK, BLOCK), 0) >= iota((BLOCK, BLOCK), 1), scores, 0.0)
+                sums = cum_v[pl.ds(pl.multiple_of(k * HEADS, HEADS), HEADS), :]
+                high, low = split_in_two(sums)
+                middle, low = split_in_two(low)
+                parts = [high, middle, low, *split_in_two(jnp.exp2(sums))]
+                columns[k] = jnp.concatenate(parts, 0).T.astype(BF16)
 
     def inside(q):
         part = lanes_of(q)
@@ -309,24 +313,24 @@
         pick = PER * q + iota((3 * HEADS, PER * BLOCK), 1) // BLOCK == iota((3 * HEADS, PER * BLOCK), 0) % HEADS
         pick = pick.astype(BF16)
 
-        @pl.loop(0, BLOCKS // 3)
+        @pl.loop(0, BLOCKS // UNROLL)
         def _(j):
-            for i in range(3):
-                k = 3 * j + i
+            for i in range(UNROLL):
+                k = UNROLL * j + i
                 rows = pl.ds(pl.multiple_of(k * BLOCK, BLOCK), BLOCK)
                 down = dot(columns[k, :, : 3 * HEADS], pick)
                 weights = []
                 for h in range(PER):
                     at = pl.ds(k * HEADS + PER * q + h, 1)
                     gap = jnp.minimum(down[:, h * BLOCK : (h + 1) * BLOCK] - cum_v[at, :], 0.0)
-                    weights.append((scores_v[k] * jnp.exp(gap) * step_v[at, :]).astype(BF16))
+                    weights.append((scores_v[k] * jnp.exp2(gap) * step_v[at, :]).astype(BF16))
                 value = xs[q, rows, :]
                 none = jnp.zeros_like(value)
                 both = jnp.concatenate([jnp.where(left, value, none), jnp.where(left, none, value)], 0)
-                y0[rows, :] = dot(jnp.concatenate(weights, 1), both) + skip_v[0:1, part] * value.astype(F32)
+                y0[q % 2, rows, :] = dot(jnp.concatenate(weights, 1), both) + skip_v[0:1, part] * value.astype(F32)
 
     def send_of(q, t, to):
-        delta = (t * t + t + 1) % 5 * (1 - t // 3)
+        delta = (4 * t * t + 2) % 5 * (1 - t // 3)
         there = (y + delta) % 4
         return pltpu.make_async_remote_copy(
             src_ref=staged.at[q, pl.ds(pl.multiple_of((2 * there + to) * TARGET, TARGET), TARGET)],
@@ -341,7 +345,7 @@
         )
 
     def scale_of(t, to):
-        delta = (t * t + t + 1) % 5 * (1 - t // 3)
+        delta = (4 * t * t + 2) % 5 * (1 - t // 3)
         there = (y + delta) % 4
         return pltpu.make_async_remote_copy(
             src_ref=scale_v.at[there], dst_ref=scale_in.at[me], send_sem=n_s.at[t, to],
@@ -368,7 +372,7 @@
 
         @pl.loop(0, 4)
         def _(t):
-            delta = (t * t + t + 1) % 5 * (1 - t // 3)
+            delta = (4 * t * t + 2) % 5 * (1 - t // 3)
             there = (y + delta) % 4
             for m in range(PASS):
                 k = PASS * there + m
@@ -377,7 +381,7 @@
                 high, low = split_in_two(state_in)
                 from_state = dot(cs[rows, :], jnp.concatenate([high, low], 0).astype(BF16))
                 decay = dot(columns[k, :, 3 * HEADS :], spread[:, part])
-                value = (y0[rows, :] + decay * from_state) * silu(gate[rows, part].astype(F32))
+                value = (y0[q % 2, rows, :] + decay * from_state) * silu(gate[rows, part].astype(F32))
                 square = jnp.where(q == 0, 0.0, squares[rows, :]) + value * value
                 squares[rows, :] = square
                 staged[q, rows, :] = (value * gain[0:1, part]).astype(BF16)
@@ -387,7 +391,7 @@
     def scales():
         @pl.loop(0, 4)
         def _(t):
-            delta = (t * t + t + 1) % 5 * (1 - t // 3)
+            delta = (4 * t * t + 2) % 5 * (1 - t // 3)
             there = (y + delta) % 4
             for m in range(PASS):
                 rows = pl.ds(pl.multiple_of((PASS * there + m) * BLOCK, BLOCK), BLOCK)
@@ -402,17 +406,30 @@
 
     loads[2].wait()
     blocks_but_first(0)
+    ahead = pl.ds(0, 2 * LEAD)
+    wide_maps[ahead, :] = jnp.zeros((2 * LEAD, STATE), F32)
+    wide[lead, :] = jnp.zeros((LEAD, WIDE), F32)
+    maps(0)
+    weights = dot(tails[0], spread[:, :WIDE])
+    value = conv(lambda r: wide[pl.ds(r, BLOCK), :], lambda tap: taps[tap : tap + 1, :WIDE]).astype(BF16)
+    xs[0, pl.ds(0, BLOCK), :] = value
+    tail = jnp.where(iota((BLOCK, WIDE), 0) < TAPS - 1, 0.0, value.astype(F32) * weights)
+    first_v[0] = dot(bt[0], tail.astype(BF16))
     for copy in halo[:2]:
         copy.wait()
-
-    @pl.when(c == 0)
-    def _():
-        bc[pl.ds(0, 2 * LEAD), :] = jnp.zeros((2 * LEAD, STATE), BF16)
-        ch[lead, pl.ds(0, WIDE)] = jnp.zeros((LEAD, WIDE), BF16)
-
-    wide_maps[pl.ds(0, 2 * LEAD), :] = bc[pl.ds(0, 2 * LEAD), :].astype(F32)
+    inner = jnp.where(c == 0, 0.0, 1.0)
+    wide_maps[ahead, :] = bc[ahead, :].astype(F32) * inner
+    wide[lead, :] = ch[lead, pl.ds(0, WIDE)].astype(F32) * inner
+    b_head = conv(
+        lambda r: wide_maps[pl.ds(2 * r, LEAD, stride=2), :], lambda tap: map_taps[tap, 0:1, :]
+    ).astype(BF16)
+    value = conv(lambda r: wide[pl.ds(r, LEAD), :], lambda tap: taps[tap : tap + 1, :WIDE]).astype(BF16)
+    xs[0, lead, :] = value
+    tail = jnp.where(iota((LEAD, WIDE), 0) < TAPS - 1, value.astype(F32) * weights[:LEAD], 0.0)
+    leave(0, first_v[0] + lax.dot_general(
+        b_head, tail.astype(BF16), (((0,), (0,)), ((), ())), preferred_element_type=F32
+    ))
     maps(0)
-    first_block(0)
     loads[3].wait()
     halo[2].wait()
 
@@ -420,38 +437,76 @@
     def _():
         ch[lead, rest] = jnp.zeros((LEAD, COLS - WIDE), BF16)
 
-    def steps(low, high, *more):
-        @pl.loop(low, high)
-        def _(q):
-            blocks_but_first(q)
-            first_block(q)
-            for what, lag in more:
-                what(q - lag)
-
-    steps(1, 3)
+    @pl.loop(1, 4)
+    def _(q):
+        blocks_but_first(q)
+        first_block(q)
+
     rings = shard_decays()
-    steps(3, 5, (along_z, 3))
-    ring_decays(rings)
-    steps(5, PARTS, (along_z, 3), (along_x, 5))
+    along_z(0)
     blocks_alone()
+
+    @pl.loop(4, 6)
+    def _(i):
+        blocks_but_first(i)
+        first_block(i)
+        along_z(i - 3)
+
+        @pl.when(i == 4)
+        def _():
+            inside(0)
+            ring_decays(rings)
+            along_x(0)
+
     loads[4].wait()
 
-    @pl.loop(0, PARTS - HELD)
-    def _(q):
-        inside(q)
-        finish(q, True)
-
-        @pl.when(q < 3)
+    exchanges = {
+        6: ((along_x, 2), (along_z, 3), (along_z, 4)),
+        7: ((along_x, 3), (along_x, 4), (along_z, 5)),
+        9: ((along_z, 6),),
+        10: ((along_z, 7),),
+    }
+    exchanges_later = {8: ((along_x, 5),), 10: ((along_x, 6),), 11: ((along_x, 7),)}
+
+    def at_step(i, step, calls):
+        @pl.when(i == step)
         def _():
-            along_z(q + PARTS - 3)
-
-        @pl.when(q < 5)
+            for what, q in calls:
+                what(q)
+
+    along_x(1)
+
+    @pl.loop(6, 13 - HELD)
+    def _(i):
+        finish(i - 6, True)
+        for step, calls in exchanges.items():
+            at_step(i, step, calls)
+        inside(i - 5)
+
+        @pl.when((i == 7) | (i == 8))
         def _():
-            along_x(q + PARTS - 5)
-
-    for q in range(PARTS - HELD, PARTS):
-        inside(q)
-        finish(q, False)
+            blocks_but_first(i - 1)
+            first_block(i - 1)
+
+        for step, calls in exchanges_later.items():
+            at_step(i, step, calls)
+
+    @pl.loop(13 - HELD, 14 - HELD)
+    def _(i):
+        finish(i - 6, True)
+
+        @pl.when(i < PARTS + 5)
+        def _():
+            inside(i - 5)
+
+    @pl.loop(14 - HELD, 14)
+    def _(i):
+        finish(i - 6, False)
+
+        @pl.when(i < PARTS + 5)
+        def _():
+            inside(i - 5)
+
     scales()
 
     @pl.loop(PARTS - HELD, PARTS)
@@ -550,7 +605,7 @@
             pltpu.VMEM((PARTS, STATE, WIDE), F32),
             pltpu.VMEM((PARTS, BLOCKS, STATE, WIDE), F32),
             pltpu.VMEM((BLOCKS, BLOCK, BLOCK), F32),
-            pltpu.VMEM((ROWS, WIDE), F32),
+            pltpu.VMEM((2, ROWS, WIDE), F32),
             pltpu.VMEM((ROWS, WIDE), F32),
             pltpu.VMEM((PARTS, ROWS, WIDE), BF16),
             pltpu.VMEM((8, PARTS, TARGET, WIDE), BF16),

time: 71.8 us -> 70 us (0.975)
  Pallas kernels: 70 us -> 68.2 us
    pallas_call x1, Pallas kernels: 70 us -> 68.2 us  [per_device(): pl.pallas_call(kernel, out_shape=pltpu.VMEM((TARGET, COLS * 8), BF16), in...]
where the time goes in v4:
time: 70 us; the launch traced here: 69.9 us
  Pallas kernels  68.2 us (97%)
  local copies, waits for them, and re-layouts  1.67 us (2%)
    pallas_call x1, Pallas kernels, per_device(): pl.pallas_call(kernel, out_shape=pltpu.VMEM((TARGET, COLS * 8), BF16), in...  68.2 us
    unnamed x1, local copies, waits for them, and re-layouts  1.67 us

profile of v4, /device:TPU:1, one launch (start us, length us, event | category | flops | bytes accessed | tf_op | source)
XLA Modules:
  0.0 69.9 jit_solution(4944032335352633499)
XLA Ops:
  0.0 68.2 %shard_map.91 = bf16[192,8192]{1,0:T(8,128)(2,1)S(1)} custom-call(bf16[1536,1024]{1,0:T(8,128)(2,1)} %ch_hbm.1, bf16[3072,128]{1,0:T(8,128)(2,1)} %bitcast.4, bf16[1536,1024]{1,0:T(8,128)(2,1)} %gate_hbm.1, f32[16,1536]{1,0:T(8,128)} %bitcast.5, f32[4,1024]{1,0:T(4,128)} %taps.1, f32[4,2,128]{2,1,0:T(2,128)} %map_taps.1, f32[2,16]{1,0:T(2,128)} %rates.1, ...), custom_call_target="tpu_custom_call" | custom-call | tf_op jit(solution)/shard_map/pallas_call | solution.py:582
  68.2 1.7 %copy.11 = bf16[192,8192]{1,0:T(8,128)(2,1)} copy(bf16[192,8192]{1,0:T(8,128)(2,1)S(1)} %shard_map.91) | data formatting | bytes 6291456

commit v5 on v4

--- a/solution.py
+++ b/solution.py
@@ -29,7 +29,7 @@
 PER = WIDE // HEAD_DIM
 PASS = 3
 HELD = 1
-UNROLL = 4
+UNROLL = 6
 
 
 def iota(shape, dim):
@@ -450,6 +450,11 @@
     def _(i):
         blocks_but_first(i)
         first_block(i)
+
+        @pl.when(i == 5)
+        def _():
+            along_x(1)
+
         along_z(i - 3)
 
         @pl.when(i == 4)
@@ -473,8 +478,6 @@
         def _():
             for what, q in calls:
                 what(q)
-
-    along_x(1)
 
     @pl.loop(6, 13 - HELD)
     def _(i):

time: 70 us -> 69.7 us (level)
  no operation moved by 1% of the time
where the time goes in v5:
time: 69.7 us; the launch traced here: 69.5 us
  Pallas kernels  67.9 us (97%)
  local copies, waits for them, and re-layouts  1.67 us (2%)
    pallas_call x1, Pallas kernels, per_device(): pl.pallas_call(kernel, out_shape=pltpu.VMEM((TARGET, COLS * 8), BF16), in...  67.9 us
    unnamed x1, local copies, waits for them, and re-layouts  1.67 us

profile of v5, /device:TPU:1, one launch (start us, length us, event | category | flops | bytes accessed | tf_op | source)
XLA Modules:
  0.0 69.5 jit_solution(10982868489627182164)
XLA Ops:
  0.0 67.9 %shard_map.91 = bf16[192,8192]{1,0:T(8,128)(2,1)S(1)} custom-call(bf16[1536,1024]{1,0:T(8,128)(2,1)} %ch_hbm.1, bf16[3072,128]{1,0:T(8,128)(2,1)} %bitcast.4, bf16[1536,1024]{1,0:T(8,128)(2,1)} %gate_hbm.1, f32[16,1536]{1,0:T(8,128)} %bitcast.5, f32[4,1024]{1,0:T(4,128)} %taps.1, f32[4,2,128]{2,1,0:T(2,128)} %map_taps.1, f32[2,16]{1,0:T(2,128)} %rates.1, ...), custom_call_target="tpu_custom_call" | custom-call | tf_op jit(solution)/shard_map/pallas_call | solution.py:585
  67.9 1.7 %copy.11 = bf16[192,8192]{1,0:T(8,128)(2,1)} copy(bf16[192,8192]{1,0:T(8,128)(2,1)S(1)} %shard_map.91) | data formatting | bytes 6291456
